TPU v7x, 512 devices: a whole 4x4x16 slice. The times are simulated.
512 devices in a mesh: tile: 64 (over z, x_hi, core), lev: 8 (over x_lo, y).
Axes of the slice: x: 4 (x_hi: 2, x_lo: 2; x = x_hi * 2 + x_lo), y: 4, z: 16, core: 2. Of those that a mesh axis runs over, the one named last changes fastest.
Arguments:
- pre_act: bfloat16 [64, 8, 64, 2304], P('tile', 'lev'), may hold values from -6 to 6
- cotangent: bfloat16 [64, 8, 2304], P('tile', 'lev'), may hold values from -6 to 6
- input_weight: bfloat16 [9, 64, 2], replicated, may hold values from -0.75 to 0.75
- conv_weight: bfloat16 [9, 64, 64], replicated, may hold values from -0.25 to 0.25
- down_weight: bfloat16 [8, 64], replicated, may hold values from -0.75 to 0.75
- level_mix: float32 [8, 8], replicated, may hold values from -2 to 2
- up_weight: bfloat16 [64, 8], replicated, may hold values from -2 to 2
- head_weight: float32 [64], replicated, may hold values from -8 to 8
- seam_list: int32 [64, 4, 3], replicated, may hold values from 0 to 63, as said below
- tile_panel: int32 [64], replicated, may hold values from 0 to 6, as said below
Outputs:
- sensitivity: float32 [64, 8, 2, 2304], P('tile', 'lev')
Inputs may be any that keep to these rules, and one draw needn't show every extreme that they name: seam_list[t, d] = (p, e, q): edge e of the tile on device p lies along side d of the tile on device t (0 start of rows, 1 end of rows, 2 start of columns, 3 end of columns), q = 1 where positions along the seam run opposite ways; the relation is symmetric, seam_list[p, e] = (t, d, q). The 54 tiles are the 3 x 3 tiles of each face of a cube, placed on devices in an order drawn from the seed; a device with no tile lists itself with edge d for side d and q = 0. `tile_panel`: panel of the tile held by each device, 6 where the device holds no tile; it agrees with seam_list.
All inputs are finite; a program needn't handle non-finite values.
Results may differ from a plain program's by a relative error of at most 0.0075.
Values may be sent and summed in bfloat16 or wider, within the bound.
A program may use at most 64 MiB of HBM per device.

v0:
```python
import jax
import jax.numpy as jnp
from jax import lax
from jax.sharding import PartitionSpec as P

TS = 48
R1 = 4
R2 = 8


def silu_grad(values):
    logistic = jax.nn.sigmoid(values)
    return logistic * (1.0 + values * (1.0 - logistic))


def edge_strips(square, rim_depth):
    upper_band = square[:, :rim_depth, :]
    lower_band = jnp.flip(square[:, -rim_depth:, :], axis=1)
    left_band = jnp.swapaxes(square[:, :, :rim_depth], 1, 2)
    right_band = jnp.flip(jnp.swapaxes(square[:, :, -rim_depth:], 1, 2), axis=1)
    return jnp.stack([upper_band, lower_band, left_band, right_band])


def orient(strips, reversal):
    turned = jnp.flip(strips, axis=3)
    return jnp.where(reversal[:, None, None, None] > 0, turned, strips)


def assemble(square, rims, rim_depth):
    channels = square.shape[0]
    upper_band = jnp.flip(rims[0], axis=1)
    left_band = jnp.swapaxes(jnp.flip(rims[2], axis=1), 1, 2)
    right_band = jnp.swapaxes(rims[3], 1, 2)
    middle = jnp.concatenate([left_band, square, right_band], axis=2)
    corner = jnp.zeros((channels, rim_depth, rim_depth), square.dtype)
    upper_rows = jnp.concatenate([corner, upper_band, corner], axis=2)
    lower_rows = jnp.concatenate([corner, rims[1], corner], axis=2)
    return jnp.concatenate([upper_rows, middle, lower_rows], axis=1)


def unassemble(joined, rim_depth, reversal):
    extent = joined.shape[1] - 2 * rim_depth
    far = rim_depth + extent
    interior = joined[:, rim_depth:far, rim_depth:far]
    upper_band = jnp.flip(joined[:, :rim_depth, rim_depth:far], axis=1)
    lower_band = joined[:, far:, rim_depth:far]
    left_band = jnp.flip(jnp.swapaxes(joined[:, rim_depth:far, :rim_depth], 1, 2), axis=1)
    right_band = jnp.swapaxes(joined[:, rim_depth:far, far:], 1, 2)
    borders = orient(jnp.stack([upper_band, lower_band, left_band, right_band]), reversal).astype(
        jnp.bfloat16
    )
    return (interior, borders)


def add_edges(interior, borders):
    extent = interior.shape[1]
    rim_depth = borders.shape[2]
    rest = extent - rim_depth
    upper_band = jnp.pad(borders[0], ((0, 0), (0, rest), (0, 0)))
    lower_band = jnp.pad(jnp.flip(borders[1], axis=1), ((0, 0), (rest, 0), (0, 0)))
    left_band = jnp.pad(jnp.swapaxes(borders[2], 1, 2), ((0, 0), (0, 0), (0, rest)))
    right_band = jnp.pad(
        jnp.swapaxes(jnp.flip(borders[3], axis=1), 1, 2), ((0, 0), (0, 0), (rest, 0))
    )
    return interior + upper_band + lower_band + left_band + right_band


def conv_forward(padded, weight, spacing):
    channels, extent = (padded.shape[0], padded.shape[1])
    out_rows = extent - 2 * spacing
    flattened = jnp.pad(padded.reshape(channels, extent * extent), ((0, 0), (spacing, spacing)))
    weight_mat = jnp.transpose(weight, (1, 0, 2)).reshape(weight.shape[1], 9 * channels)
    stride = out_rows // 4
    outputs = []
    for block_index in range(4):
        anchor = (block_index * stride + spacing) * extent + spacing
        shifted = []
        for row_step in (-1, 0, 1):
            for col_step in (-1, 0, 1):
                opening = anchor + row_step * spacing * extent + col_step * spacing
                shifted.append(
                    lax.slice_in_dim(flattened, opening, opening + stride * extent, axis=1)
                )
        stacked = jnp.concatenate(shifted, axis=0)
        outputs.append(jnp.dot(weight_mat, stacked, preferred_element_type=jnp.float32))
    joined = jnp.concatenate(outputs, axis=1).reshape(weight.shape[1], out_rows, extent)
    return joined[:, :, spacing : spacing + out_rows]


def route_strips(strips, seam_list):
    flattened = strips.reshape(4, -1)
    pieces_in = lax.all_to_all(flattened, "tile", split_axis=1, concat_axis=0, tiled=True)
    wanted = (seam_list[:, :, 0] * 4 + seam_list[:, :, 1]).reshape(-1)
    picked = jnp.take(pieces_in, wanted, axis=0)
    arrived = lax.all_to_all(picked, "tile", split_axis=0, concat_axis=1, tiled=True)
    return arrived.reshape(strips.shape)


def mix_levels(latents, matrix):
    level_index = lax.axis_index("lev")
    coeffs = lax.dynamic_index_in_dim(matrix, level_index, 0, keepdims=False)
    running = jnp.einsum(
        "n,nzc->zc",
        coeffs,
        lax.all_gather(latents[None], "lev", axis=0, tiled=True).astype(jnp.float32),
        precision=lax.Precision.HIGHEST,
    )
    result = running.astype(jnp.bfloat16)
    return result


def shards(
    pre_act,
    cotangent,
    input_weight,
    conv_weight,
    down_weight,
    level_mix,
    up_weight,
    head_weight,
    seam_list,
    tile_panel,
):
    position = lax.axis_index("tile")
    own_seam = lax.dynamic_index_in_dim(seam_list, position, 0, keepdims=False)
    reversal = own_seam[:, 2]
    hidden = pre_act.shape[2]
    pre_wide = pre_act[0, 0].astype(jnp.float32)
    first_act = jax.nn.silu(pre_wide).astype(jnp.bfloat16).reshape(hidden, TS, TS)
    rims = route_strips(edge_strips(first_act, R2), seam_list)
    padded = assemble(first_act, orient(rims, reversal), R2)
    second_pre = conv_forward(padded, conv_weight, R2).reshape(hidden, TS * TS)
    second_act = jax.nn.silu(second_pre).astype(jnp.bfloat16)
    latents = jnp.dot(down_weight, second_act, preferred_element_type=jnp.float32).astype(
        jnp.bfloat16
    )
    mixture = mix_levels(latents, level_mix)
    third_act = second_act.astype(jnp.float32) + jnp.dot(
        up_weight, mixture, preferred_element_type=jnp.float32
    )
    top_grad = (
        cotangent[0, 0].astype(jnp.float32)[None, :] * head_weight[:, None] * silu_grad(third_act)
    )
    contract = (((0,), (0,)), ((), ()))
    latent_grad = lax.dot_general(
        up_weight, top_grad.astype(jnp.bfloat16), contract, preferred_element_type=jnp.float32
    ).astype(jnp.bfloat16)
    mixed_grad = mix_levels(latent_grad, level_mix.T)
    second_grad = top_grad + lax.dot_general(
        down_weight, mixed_grad, contract, preferred_element_type=jnp.float32
    )
    deep_grad = (second_grad * silu_grad(second_pre)).astype(jnp.bfloat16).reshape(hidden, TS, TS)
    margin = 2 * R2
    padded_grad = conv_forward(
        jnp.pad(deep_grad, ((0, 0), (margin, margin), (margin, margin))),
        jnp.swapaxes(conv_weight[::-1], 1, 2),
        R2,
    )
    interior, borders = unassemble(padded_grad, R2, reversal)
    first_grad = add_edges(interior, route_strips(borders, seam_list).astype(jnp.float32)).reshape(
        hidden, TS * TS
    )
    shallow_grad = (first_grad * silu_grad(pre_wide)).astype(jnp.bfloat16).reshape(hidden, TS, TS)
    margin_in = 2 * R1
    input_grad = conv_forward(
        jnp.pad(shallow_grad, ((0, 0), (margin_in, margin_in), (margin_in, margin_in))),
        jnp.swapaxes(input_weight[::-1], 1, 2),
        R1,
    )
    interior_in, borders_in = unassemble(input_grad, R1, reversal)
    result = add_edges(interior_in, route_strips(borders_in, seam_list).astype(jnp.float32))
    active = (lax.dynamic_index_in_dim(tile_panel, position, 0, keepdims=False) < 6).astype(
        jnp.float32
    )
    return (result * active).reshape(1, 1, 2, TS * TS)


def solution(mesh):
    return jax.shard_map(
        shards,
        mesh=mesh,
        in_specs=(
            P("tile", "lev", None, None),
            P("tile", "lev", None),
            P(),
            P(),
            P(),
            P(),
            P(),
            P(),
            P(),
            P(),
        ),
        out_specs=P("tile", "lev", None, None),
        check_vma=False,
    )
```

profile of v0, /device:TPU:1, one launch (start us, length us, event | category | flops | bytes accessed | tf_op | source)
XLA Modules:
  0.0 275.9 jit_solution(13281421134178905453)
XLA Ops:
  0.0 2.0 reshape.208
  2.0 0.4 multiply_convert_fusion
  2.4 1.2 slice_bitcast_fusion.1
  3.9 1.4 copy.138
  5.5 2.9 %rev.58 = bf16[64,8,48]{1,2,0:T(8,128)(2,1)S(1)} reverse(bf16[64,8,48]{1,2,0:T(8,128)(2,1)S(1)} %get-tuple-element.32), dimensions={1} | reverse | bytes 98304 | tf_op jit(solution)/shard_map/jit(_flip)/rev | solution.py:20
  8.8 0.8 copy.140
  9.7 19.6 %all-to-all-start = ((bf16[4,64,384]{2,0,1:T(4,128)(2,1)}), bf16[4,64,384]{2,0,1:T(4,128)(2,1)S(1)}, u32[]{:S(2)}, u32[]{:S(2)}) async-start(bf16[4,64,384]{2,0,1:T(4,128)(2,1)} %copy.140), calls=%async_computation | async-start | bytes 393216 | tf_op jit(solution)/shard_map/all_to_all | solution.py:92
  29.6 20.8 %all-to-all-done = bf16[4,64,384]{2,0,1:T(4,128)(2,1)S(1)} async-done(((bf16[4,64,384]{2,0,1:T(4,128)(2,1)}), bf16[4,64,384]{2,0,1:T(4,128)(2,1)S(1)}, u32[]{:S(2)}, u32[]{:S(2)}) %all-to-all-start) | async-done | bytes 196640 | tf_op jit(solution)/shard_map/all_to_all | solution.py:92
  50.5 1.2 gather_fusion.1
  51.8 0.7 all_to_all.73
  52.5 4.4 %all-to-all-start.1 = ((bf16[64,4,384]{2,1,0:T(4,128)(2,1)}), bf16[64,4,384]{2,1,0:T(4,128)(2,1)S(1)}, u32[]{:S(2)}, u32[]{:S(2)}) async-start(bf16[64,4,384]{2,1,0:T(4,128)(2,1)} %all_to_all.73), calls=%async_computation.1 | async-start | bytes 393216 | tf_op jit(solution)/shard_map/all_to_all | solution.py:95
  57.7 20.3 %all-to-all-done.1 = bf16[64,4,384]{2,1,0:T(4,128)(2,1)S(1)} async-done(((bf16[64,4,384]{2,1,0:T(4,128)(2,1)}), bf16[64,4,384]{2,1,0:T(4,128)(2,1)S(1)}, u32[]{:S(2)}, u32[]{:S(2)}) %all-to-all-start.1) | async-done | bytes 196640 | tf_op jit(solution)/shard_map/all_to_all | solution.py:95
  78.3 0.5 rev.59
  79.2 0.6 copy.145
  79.9 1.5 copy.146
  81.4 2.1 maximum_maximum_fusion
  83.5 0.8 reshape.195
  85.5 0.3 convolution_bitcast_fusion.9
  85.9 0.3 convolution_bitcast_fusion.6
  86.2 0.3 convolution_bitcast_fusion.7
  86.6 0.3 convolution_bitcast_fusion.8
  87.0 0.4 reshape.197
  87.4 0.5 slice.690
  87.9 0.7 reshape.198
  88.9 22.1 %all-gather = bf16[64,2304]{1,0:T(8,128)(2,1)S(1)} all-gather(bf16[8,2304]{1,0:T(8,128)(2,1)S(1)} %fusion.4), channel_id=2, replica_groups=mesh['tile'=64,'lev'=8] {'lev'}, dimensions={0}, use_global_device_ids=true | all-gather | bytes 331776 | tf_op jit(solution)/shard_map/all_gather | solution.py:105
  111.0 0.4 fusion.13
  111.4 0.4 multiply_multiply_fusion
  112.0 22.6 %all-gather.1 = bf16[64,2304]{1,0:T(8,128)(2,1)S(1)} all-gather(bf16[8,2304]{1,0:T(8,128)(2,1)S(1)} %fusion.5), channel_id=3, replica_groups=mesh['tile'=64,'lev'=8] {'lev'}, dimensions={0}, use_global_device_ids=true | all-gather | bytes 331776 | tf_op jit(solution)/shard_map/all_gather | solution.py:105
  134.6 0.4 fusion.11
  135.0 0.4 fusion.3
  135.4 1.1 reshape.199
  136.5 0.3 pad.53
  136.8 1.4 reshape.200
  139.6 0.4 convolution_bitcast_fusion.5
  140.2 0.4 convolution_bitcast_fusion.4
  141.2 0.4 convolution_bitcast_fusion.3
  142.2 0.4 convolution_bitcast_fusion.2
  142.7 1.0 reshape.202
  143.9 1.3 fusion.25
  145.6 1.8 copy.176
  147.4 0.7 copy.177
  148.2 0.5 rev.65
  149.1 37.5 %all_to_all.93 = bf16[4,64,384]{2,0,1:T(4,128)(2,1)S(1)} all-to-all(bf16[4,64,384]{2,0,1:T(4,128)(2,1)S(1)} %copy.154), channel_id=1, replica_groups=mesh['tile'=64,'lev'=8] {'tile'}, dimensions={1} | all-to-all | bytes 393216 | tf_op jit(solution)/shard_map/all_to_all | solution.py:92
  186.6 1.2 gather_fusion.2
  187.9 0.7 all_to_all.80
  188.7 4.4 %all-to-all-start.3 = ((bf16[64,4,384]{2,1,0:T(4,128)(2,1)}), bf16[64,4,384]{2,1,0:T(4,128)(2,1)S(1)}, u32[]{:S(2)}, u32[]{:S(2)}) async-start(bf16[64,4,384]{2,1,0:T(4,128)(2,1)} %all_to_all.80), calls=%async_computation.3 | async-start | bytes 393216 | tf_op jit(solution)/shard_map/all_to_all | solution.py:95
  193.3 20.9 %all-to-all-done.3 = bf16[64,4,384]{2,1,0:T(4,128)(2,1)S(1)} async-done(((bf16[64,4,384]{2,1,0:T(4,128)(2,1)}), bf16[64,4,384]{2,1,0:T(4,128)(2,1)S(1)}, u32[]{:S(2)}, u32[]{:S(2)}) %all-to-all-start.3) | async-done | bytes 196640 | tf_op jit(solution)/shard_map/all_to_all | solution.py:95
  214.3 1.0 slice_reduce_fusion.3
  215.9 1.6 copy.155
  217.5 1.7 copy.156
  219.2 3.6 %rev.67 = f32[64,8,48]{1,2,0:T(8,128)} reverse(f32[64,8,48]{1,2,0:T(8,128)} %copy.156), dimensions={1} | reverse | bytes 196608 | tf_op jit(solution)/shard_map/jit(_flip)/rev | solution.py:63
  222.9 3.3 %fusion.10 = bf16[64,48,48]{2,1,0:T(8,128)(2,1)S(1)} fusion(f32[64,64,80]{2,1,0:T(8,128)S(1)} %reshape.202, f32[64,48,48]{2,1,0:T(8,128)} %copy-done.1, f32[64,48,8]{2,1,0:T(8,128)} %bitcast.160, f32[64,48,8]{2,1,0:T(8,128)} %bitcast.159, f32[64,8,48]{2,1,0:T(8,128)S(1)} %rev.66, f32[64,8,48]{2,1,0:T(8,128)S(1)} %squeeze.64), kind=kLoop, calls=%fused_computation.22 | loop fusion | flops 1916928 | bytes 1867776 | tf_op jit(solution)/shard_map/convert_element_type | solution.py:163
  226.2 0.3 pad.59
  226.5 0.8 reshape.203
  230.7 0.7 copy.161
  231.4 4.2 %all-to-all-start.4 = ((bf16[4,64,6]{2,0,1:T(4,128)(2,1)}), bf16[4,64,6]{2,0,1:T(4,128)(2,1)S(1)}, u32[]{:S(2)}, u32[]{:S(2)}) async-start(bf16[4,64,6]{2,0,1:T(4,128)(2,1)} %copy.161), calls=%async_computation.4 | async-start | bytes 131072 | tf_op jit(solution)/shard_map/all_to_all | solution.py:92
  235.7 15.7 %all-to-all-done.4 = bf16[4,64,6]{2,0,1:T(4,128)(2,1)S(1)} async-done(((bf16[4,64,6]{2,0,1:T(4,128)(2,1)}), bf16[4,64,6]{2,0,1:T(4,128)(2,1)S(1)}, u32[]{:S(2)}, u32[]{:S(2)}) %all-to-all-start.4) | async-done | bytes 3104 | tf_op jit(solution)/shard_map/all_to_all | solution.py:92
  251.4 0.9 gather_fusion
  252.3 0.8 broadcast_select_fusion.3
  253.0 4.4 %all-to-all-start.5 = ((bf16[64,4,6]{2,1,0:T(4,128)(2,1)}), bf16[64,4,6]{2,1,0:T(4,128)(2,1)S(1)}, u32[]{:S(2)}, u32[]{:S(2)}) async-start(bf16[64,4,6]{2,1,0:T(4,128)(2,1)} %broadcast_select_fusion.3), calls=%async_computation.5 | async-start | bytes 131072 | tf_op jit(solution)/shard_map/all_to_all | solution.py:95
  257.5 0.6 dynamic_slice.15
  258.7 14.9 %all-to-all-done.5 = bf16[64,4,6]{2,1,0:T(4,128)(2,1)S(1)} async-done(((bf16[64,4,6]{2,1,0:T(4,128)(2,1)}), bf16[64,4,6]{2,1,0:T(4,128)(2,1)S(1)}, u32[]{:S(2)}, u32[]{:S(2)}) %all-to-all-start.5) | async-done | bytes 3104 | tf_op jit(solution)/shard_map/all_to_all | solution.py:95
  273.6 0.4 slice_reduce_fusion.7
  274.8 0.7 reshape.206
  (152 shorter events, 13.2 us)
Async XLA Ops:
  0.0 57.2 %copy-start = (f32[8,8]{1,0:T(8,128)S(1)}, f32[8,8]{1,0:T(8,128)}, u32[]{:S(2)}) copy-start(f32[8,8]{1,0:T(8,128)} %param.17) | copy-start | bytes 772
  2.0 1.6 copy-start.1
  8.4 21.0 %copy-start.3 = (s32[64,4,3]{0,1,2:T(4,128)S(1)}, s32[64,4,3]{0,1,2:T(4,128)}, u32[]{:S(2)}) copy-start(s32[64,4,3]{0,1,2:T(4,128)} %param.20) | copy-start | bytes 9220
  9.7 40.7 %all-to-all-start = ((bf16[4,64,384]{2,0,1:T(4,128)(2,1)}), bf16[4,64,384]{2,0,1:T(4,128)(2,1)S(1)}, u32[]{:S(2)}, u32[]{:S(2)}) async-start(bf16[4,64,384]{2,0,1:T(4,128)(2,1)} %copy.140), calls=%async_computation | async-start | bytes 393216 | tf_op jit(solution)/shard_map/all_to_all | solution.py:92
  50.5 6.6 %copy-start.2 = (bf16[9,64,64]{2,1,0:T(8,128)(2,1)S(1)}, bf16[9,64,64]{2,1,0:T(8,128)(2,1)}, u32[]{:S(2)}) copy-start(bf16[9,64,64]{2,1,0:T(8,128)(2,1)} %param.15) | copy-start | bytes 221188
  50.5 7.2 %copy-start.4 = (bf16[1,1,2304]{2,1,0:T(2,128)(2,1)S(1)}, bf16[1,1,2304]{2,1,0:T(2,128)(2,1)}, u32[]{:S(2)}) copy-start(bf16[1,1,2304]{2,1,0:T(2,128)(2,1)} %param.13) | copy-start | bytes 13828
  52.5 25.5 %all-to-all-start.1 = ((bf16[64,4,384]{2,1,0:T(4,128)(2,1)}), bf16[64,4,384]{2,1,0:T(4,128)(2,1)S(1)}, u32[]{:S(2)}, u32[]{:S(2)}) async-start(bf16[64,4,384]{2,1,0:T(4,128)(2,1)} %all_to_all.73), calls=%async_computation.1 | async-start | bytes 393216 | tf_op jit(solution)/shard_map/all_to_all | solution.py:95
  87.9 0.9 copy-start.7
  88.6 22.8 %copy-start.6 = (bf16[64,8]{0,1:T(8,128)(2,1)S(1)}, bf16[64,8]{0,1:T(8,128)(2,1)}, u32[]{:S(2)}) copy-start(bf16[64,8]{0,1:T(8,128)(2,1)} %param.18) | copy-start | bytes 3076
  88.6 22.8 %copy-start.8 = (f32[64]{0:T(128)S(1)}, f32[64]{0:T(128)}, u32[]{:S(2)}) copy-start(f32[64]{0:T(128)} %param.19) | copy-start | bytes 772
  186.6 6.6 %copy-start.5 = (bf16[9,64,2]{1,2,0:T(2,128)(2,1)S(1)}, bf16[9,64,2]{1,2,0:T(2,128)(2,1)}, u32[]{:S(2)}) copy-start(bf16[9,64,2]{1,2,0:T(2,128)(2,1)} %param.14) | copy-start | bytes 6916
  188.7 25.6 %all-to-all-start.3 = ((bf16[64,4,384]{2,1,0:T(4,128)(2,1)}), bf16[64,4,384]{2,1,0:T(4,128)(2,1)S(1)}, u32[]{:S(2)}, u32[]{:S(2)}) async-start(bf16[64,4,384]{2,1,0:T(4,128)(2,1)} %all_to_all.80), calls=%async_computation.3 | async-start | bytes 393216 | tf_op jit(solution)/shard_map/all_to_all | solution.py:95
  229.6 27.9 %copy-start.9 = (s32[64]{0:T(128)S(1)}, s32[64]{0:T(128)}, u32[]{:S(2)}) copy-start(s32[64]{0:T(128)} %param.21) | copy-start | bytes 772
  231.4 20.0 %all-to-all-start.4 = ((bf16[4,64,6]{2,0,1:T(4,128)(2,1)}), bf16[4,64,6]{2,0,1:T(4,128)(2,1)S(1)}, u32[]{:S(2)}, u32[]{:S(2)}) async-start(bf16[4,64,6]{2,0,1:T(4,128)(2,1)} %copy.161), calls=%async_computation.4 | async-start | bytes 131072 | tf_op jit(solution)/shard_map/all_to_all | solution.py:92
  253.0 20.6 %all-to-all-start.5 = ((bf16[64,4,6]{2,1,0:T(4,128)(2,1)}), bf16[64,4,6]{2,1,0:T(4,128)(2,1)S(1)}, u32[]{:S(2)}, u32[]{:S(2)}) async-start(bf16[64,4,6]{2,1,0:T(4,128)(2,1)} %broadcast_select_fusion.3), calls=%async_computation.5 | async-start | bytes 131072 | tf_op jit(solution)/shard_map/all_to_all | solution.py:95
where the time goes:
time: 281 us; the launch traced here: 276 us
  waiting for transfers between devices  92.6 us (33%)
  blocking collectives  82.2 us (29%)
  local copies, waits for them, and re-layouts  48 us (17%)
  starting transfers between devices  37 us (13%)
  other arithmetic  8.04 us (3%)
  matrix products  5.98 us (2%)
    all_to_all x3, waiting for transfers between devices, route_strips(): lax.all_to_all(picked, 'tile', split_axis=0, concat_axis=1, tiled=True)  56.1 us
    all_gather x2, blocking collectives, mix_levels(): lax.all_gather(latents[None], 'lev', axis=0, tiled=True).astype(jnp.float32)  44.7 us
    all_to_all x1, blocking collectives, route_strips(): lax.all_to_all(flattened, 'tile', split_axis=1, concat_axis=0, tiled=True)  37.5 us
    all_to_all x2, waiting for transfers between devices, route_strips(): lax.all_to_all(flattened, 'tile', split_axis=1, concat_axis=0, tiled=True)  36.5 us
    all_to_all x2, starting transfers between devices, route_strips(): lax.all_to_all(flattened, 'tile', split_axis=1, concat_axis=0, tiled=True)  23.8 us
    all_to_all x3, starting transfers between devices, route_strips(): lax.all_to_all(picked, 'tile', split_axis=0, concat_axis=1, tiled=True)  13.2 us
    unnamed x66, local copies, waits for them, and re-layouts  6.95 us
  transfers between devices with their start and end apart: 5, of which 5 were waited for; matrix products, arithmetic and copies ran while one was open for 1% of the time, Pallas kernels for 0%

commit v1 on v0

v1 whole, which is shorter than its diff:
```python
import functools

import jax
import jax.numpy as jnp
from jax import lax
from jax.experimental import pallas as pl
from jax.experimental.pallas import tpu as pltpu
from jax.sharding import PartitionSpec as P

F32 = jnp.float32
BF16 = jnp.bfloat16
MESH = pl.DeviceIdType.MESH
NT = (((1,), (1,)), ((), ()))
NN = (((1,), (0,)), ((), ()))
TILES = 64
LEVS = 8


def dot(a, b, dims=NN):
    return lax.dot_general(a, b, dims, preferred_element_type=F32)


def dsilu(v):
    g = jax.nn.sigmoid(v)
    return g * (1.0 + v * (1.0 - g))


def iota(shape, axis):
    return lax.broadcasted_iota(jnp.int32, shape, axis)


def rows_from_pieces(rows, pieces):
    view = rows.reshape(3, 32, 8, 128)

    def step(m, carry):
        for h in range(2):
            for j in range(3):
                view[j, m, 4 * h : 4 * h + 4, :] = pieces[2 * m + h, j].astype(F32)
        return carry

    lax.fori_loop(0, 32, step, 0)


def pieces_from_rows(pieces, rows):
    view = rows.reshape(3, 32, 8, 128)

    def step(m, carry):
        for h in range(2):
            for j in range(3):
                pieces[2 * m + h, j] = view[j, m, 4 * h : 4 * h + 4, :].astype(BF16)
        return carry

    lax.fori_loop(0, 32, step, 0)


def rows_from_slab(rows, member, slab):
    for j in range(3):
        block = jnp.concatenate([slab[128 * j : 128 * j + 64], slab[128 * j + 64 : 128 * j + 128]], axis=1)
        rows[j, pl.ds(member, 64, stride=4), :] = block


def slab_from_rows(rows, member):
    parts = []
    for j in range(3):
        block = rows[j, pl.ds(member, 64, stride=4), :]
        parts += [block[:, :64], block[:, 64:]]
    return jnp.concatenate(parts, axis=0)


def spread_start(send, recv, send_sem, recv_sem, me):
    recv[me] = send[me]

    def step(i, carry):
        target = lax.rem(me + i, TILES)
        pltpu.make_async_remote_copy(
            send.at[target], recv.at[me], send_sem, recv_sem,
            device_id={"tile": target}, device_id_type=MESH,
        ).start()
        return carry

    lax.fori_loop(1, TILES, step, 0)


def spread_wait(send, recv, send_sem, recv_sem):
    others = pl.ds(0, TILES - 1)
    pltpu.make_async_copy(recv.at[others], recv.at[others], recv_sem).wait()
    pltpu.make_async_copy(send.at[others], send.at[others], send_sem).wait()


def level_start(buf, send_sem, recv_sem, level):
    for i in range(1, LEVS):
        pltpu.make_async_remote_copy(
            buf.at[level], buf.at[level], send_sem, recv_sem,
            device_id={"lev": lax.rem(level + i, LEVS)}, device_id_type=MESH,
        ).start()


def level_wait(buf, send_sem, recv_sem):
    others = pl.ds(0, LEVS - 1)
    pltpu.make_async_copy(buf.at[others], buf.at[others], recv_sem).wait()
    pltpu.make_async_copy(buf.at[others], buf.at[others], send_sem).wait()


def pick(rows, choice):
    for j in range(3):
        rows[j] = dot(choice, rows[j].astype(BF16))


def turn_matrix(side, edge, flip, of_bands):
    if side < 2:
        r, b = iota((8, 48, 128), 0), iota((8, 48, 128), 1)
    else:
        b, r = iota((48, 8, 128), 0), iota((48, 8, 128), 1)
    r, b = r.reshape(384, 128), b.reshape(384, 128)
    turned_here = (side % 2 == 0) if not of_bands else (side % 2 == 1)
    a = 7 - r if turned_here else r
    odd = lax.rem(edge, 2)
    turned_there = odd if not of_bands else 1 - odd
    depth = turned_there * 7 + (1 - 2 * turned_there) * a
    along = flip * 47 + (1 - 2 * flip) * b
    by_rows = jnp.where(edge < 2, 1, 0)
    index = depth * (1 + 47 * by_rows) + along * (8 - 7 * by_rows)
    lanes = iota((384, 128), 1)
    return jnp.concatenate(
        [jnp.where(index == lanes + 128 * j, 1.0, 0.0).astype(BF16) for j in range(3)], axis=1
    )


def kernel(
    pre_ref, cot_ref, in_w, conv_w, down_ref, mix_ref, up_ref, head_ref, seam, seam_v, panel, out_ref,
    pre_t, padded, wide, act, second, top, deep_wide, grad, shallow, bands_t, turns, place, rows, wanted,
    choice, a_send, a_recv, b_send, b_recv, c_send, c_recv, d_send, d_recv, e_send, e_recv, lat, glat,
    send_sem, recv_sem,
):
    me = lax.axis_index("tile")
    level = lax.axis_index("lev")
    barrier = pltpu.get_barrier_semaphore()

    def greet(i, carry):
        pl.semaphore_signal(barrier, inc=1, device_id={"tile": lax.rem(me + i, TILES)}, device_id_type=MESH)
        return carry

    lax.fori_loop(1, TILES, greet, 0)
    for i in range(1, LEVS):
        pl.semaphore_signal(barrier, inc=1, device_id={"lev": lax.rem(level + i, LEVS)}, device_id_type=MESH)

    pre_t[...] = pre_ref[0, 0].astype(F32).T.reshape(48, 48, 64)
    padded[0:8] = jnp.zeros((8, 64, 64), F32)
    padded[56:64] = jnp.zeros((8, 64, 64), F32)

    def first(c, carry):
        v = pre_t[pl.ds(8 * c, 8)]
        s = v * jax.nn.sigmoid(v)
        padded[pl.ds(8 * c + 8, 8), 8:56, :] = s.astype(BF16).astype(F32)
        return carry

    lax.fori_loop(0, 6, first, 0)
    rows_from_slab(rows, 0, padded[8:16, 8:56, :].reshape(384, 64))
    rows_from_slab(rows, 1, padded[48:56, 8:56, :].reshape(384, 64))
    rows_from_slab(rows, 2, padded[8:56, 8:16, :].reshape(384, 64))
    rows_from_slab(rows, 3, padded[8:56, 48:56, :].reshape(384, 64))
    pieces_from_rows(a_send, rows)
    pl.semaphore_wait(barrier, TILES - 1 + LEVS - 1)
    spread_start(a_send, a_recv, send_sem.at[0], recv_sem.at[0], me)

    wide_view = wanted.reshape(32, 8, 3)

    def want(m, carry):
        for h in range(2):
            wide_view[m, 4 * h : 4 * h + 4, :] = seam_v[2 * m + h]
        return carry

    lax.fori_loop(0, 32, want, 0)
    table = wanted[...]
    wished = table[:, 0:1] * 4 + table[:, 1:2]
    for j in range(2):
        choice[:, 128 * j : 128 * j + 128] = jnp.where(
            wished == iota((256, 128), 1) + 128 * j, 1.0, 0.0
        ).astype(BF16)
    for side in range(4):
        turns[0, side] = turn_matrix(side, seam[me, side, 1], seam[me, side, 2], False)

    spread_wait(a_send, a_recv, send_sem.at[0], recv_sem.at[0])
    rows_from_pieces(rows, a_recv)
    pick(rows, choice[...])
    pieces_from_rows(b_send, rows)
    spread_start(b_send, b_recv, send_sem.at[1], recv_sem.at[1], me)

    for side in range(4):
        turns[1, side] = turn_matrix(side, seam[me, side, 1], seam[me, side, 2], True)

    spread_wait(b_send, b_recv, send_sem.at[1], recv_sem.at[1])
    rows_from_pieces(rows, b_recv)
    rims = [dot(turns[0, side], slab_from_rows(rows, side).astype(BF16)) for side in range(4)]
    padded[0:8, 8:56, :] = rims[0].reshape(8, 48, 64)
    padded[56:64, 8:56, :] = rims[1].reshape(8, 48, 64)
    padded[8:56, 0:8, :] = rims[2].reshape(48, 8, 64)
    padded[8:56, 56:64, :] = rims[3].reshape(48, 8, 64)

    def widen(c, carry):
        x = padded[pl.ds(8 * c, 8)]
        wide[pl.ds(8 * c, 8)] = jnp.concatenate([x[:, 0:48], x[:, 8:56], x[:, 16:64]], axis=2).astype(BF16)
        return carry

    lax.fori_loop(0, 8, widen, 0)
    down = down_ref[...]
    up = up_ref[...]
    forward = [
        jnp.concatenate([conv_w[3 * a + b] for b in range(3)], axis=1) for a in range(3)
    ]

    def conv(c, carry):
        total = jnp.zeros((384, 64), F32)
        for a in range(3):
            total += dot(wide[pl.ds(8 * (c + a), 8)].reshape(384, 192), forward[a], NT)
        second[c] = total
        s = (total * jax.nn.sigmoid(total)).astype(BF16)
        act[c] = s
        lat[level, c] = dot(down, s, NT).astype(BF16)
        return carry

    lax.fori_loop(0, 6, conv, 0)
    level_start(lat, send_sem.at[2], recv_sem.at[2], level)

    head = head_ref[...]
    high = head.astype(BF16)
    rest = head - high.astype(F32)
    middle = rest.astype(BF16)
    low = (rest - middle.astype(F32)).astype(BF16)
    zero_rows = jnp.zeros((5, 64), F32)
    heads = jnp.concatenate(
        [high.astype(F32), middle.astype(F32), low.astype(F32), zero_rows], axis=0
    ).astype(BF16)
    eye = jnp.where(iota((8, 8), 0) == iota((8, 8), 1), 1.0, 0.0).astype(BF16)
    up_t = dot(eye, up, NT).astype(BF16)

    level_wait(lat, send_sem.at[2], recv_sem.at[2])

    def top_step(c, carry):
        mixed = mix_ref[level, 0] * lat[0, c].astype(F32)
        for other in range(1, LEVS):
            mixed += mix_ref[level, other] * lat[other, c].astype(F32)
        mixed = mixed.astype(BF16).astype(F32).T.astype(BF16)
        third = act[c].astype(F32) + dot(mixed, up, NT)
        cot = jnp.broadcast_to(cot_ref[c].astype(F32), (8, 384)).T.astype(BF16)
        gradient = dot(cot, heads) * dsilu(third)
        top[c] = gradient
        glat[level, c] = dot(up_t, gradient.astype(BF16), NT).astype(BF16)
        return carry

    lax.fori_loop(0, 6, top_step, 0)
    level_start(glat, send_sem.at[3], recv_sem.at[3], level)

    def clear(c, carry):
        deep_wide[pl.ds(8 * c, 8)] = jnp.zeros((8, 64, 192), BF16)
        deep_wide[pl.ds(64 + 8 * c, 8)] = jnp.zeros((8, 64, 192), BF16)
        return carry

    lax.fori_loop(0, 2, clear, 0)
    shallow[0:8] = jnp.zeros((8, 48, 64), BF16)
    shallow[56:64] = jnp.zeros((8, 48, 64), BF16)
    level_wait(glat, send_sem.at[3], recv_sem.at[3])

    def deep_step(c, carry):
        mixed = mix_ref[0, level] * glat[0, c].astype(F32)
        for other in range(1, LEVS):
            mixed += mix_ref[other, level] * glat[other, c].astype(F32)
        mixed = mixed.astype(BF16).astype(F32).T.astype(BF16)
        gradient = top[c] + dot(mixed, down)
        d = (gradient * dsilu(second[c])).reshape(8, 48, 64)
        z8 = jnp.zeros((8, 8, 64), F32)
        z16 = jnp.zeros((8, 16, 64), F32)
        joined = jnp.concatenate(
            [
                jnp.concatenate([d, z16], axis=1),
                jnp.concatenate([z8, d, z8], axis=1),
                jnp.concatenate([z16, d], axis=1),
            ],
            axis=2,
        )
        deep_wide[pl.ds(8 * c + 16, 8)] = joined.astype(BF16)
        return carry

    lax.fori_loop(0, 6, deep_step, 0)
    backward = [conv_w[3 * a : 3 * a + 3].reshape(192, 64) for a in range(3)]

    def adjoint(c, carry):
        total = jnp.zeros((512, 64), F32)
        for a in range(3):
            total += dot(deep_wide[pl.ds(8 * (c + 2 - a), 8)].reshape(512, 192), backward[a])
        grad[pl.ds(8 * c, 8)] = total.reshape(8, 64, 64)
        return carry

    lax.fori_loop(0, 8, adjoint, 0)
    rows_from_slab(rows, 0, grad[0:8, 8:56, :].reshape(384, 64))
    rows_from_slab(rows, 1, grad[56:64, 8:56, :].reshape(384, 64))
    rows_from_slab(rows, 2, grad[8:56, 0:8, :].reshape(384, 64))
    rows_from_slab(rows, 3, grad[8:56, 56:64, :].reshape(384, 64))
    pieces_from_rows(c_send, rows)
    spread_start(c_send, c_recv, send_sem.at[4], recv_sem.at[4], me)

    def slope(c, carry):
        pre_t[pl.ds(8 * c, 8)] = dsilu(pre_t[pl.ds(8 * c, 8)])
        return carry

    lax.fori_loop(0, 6, slope, 0)
    cell = iota((8, 2304), 1)
    row = jnp.zeros((8, 2304), jnp.int32)
    for i in range(1, 48):
        row += jnp.where(cell >= 48 * i, 1, 0)
    column = cell - 48 * row
    for side in range(4):
        edge, flip = seam[me, side, 1], seam[me, side, 2]
        a, b = [(row, column), (47 - row, column), (column, row), (47 - column, row)][side]
        turned = 1 - lax.rem(edge, 2)
        by_rows = jnp.where(edge < 2, 1, 0)
        depth = turned * 3 + (1 - 2 * turned) * a
        along = flip * 47 + (1 - 2 * flip) * b
        index = depth * (1 + 47 * by_rows) + along * (4 - 3 * by_rows)
        index = jnp.where(a < 4, index, -1)

        def put(k, carry, side=side, index=index):
            base = pl.multiple_of(16 * k, 16)
            low_half = jnp.where(index == iota((8, 2304), 0) + base, 1.0, 0.0)
            high_half = jnp.where(index == iota((8, 2304), 0) + base + 8, 1.0, 0.0)
            place[pl.ds(pl.multiple_of(192 * side + base, 16), 16), :] = jnp.concatenate(
                [low_half, high_half], axis=0
            ).astype(BF16)
            return carry

        lax.fori_loop(0, 12, put, 0)

    spread_wait(c_send, c_recv, send_sem.at[4], recv_sem.at[4])
    rows_from_pieces(rows, c_recv)
    pick(rows, choice[...])
    pieces_from_rows(d_send, rows)
    spread_start(d_send, d_recv, send_sem.at[5], recv_sem.at[5], me)
    spread_wait(d_send, d_recv, send_sem.at[5], recv_sem.at[5])
    rows_from_pieces(rows, d_recv)
    rims = [dot(turns[1, side], slab_from_rows(rows, side).astype(BF16)) for side in range(4)]
    grad[8:16, 8:56, :] += rims[0].reshape(8, 48, 64)
    grad[48:56, 8:56, :] += rims[1].reshape(8, 48, 64)
    grad[8:56, 8:16, :] += rims[2].reshape(48, 8, 64)
    grad[8:56, 48:56, :] += rims[3].reshape(48, 8, 64)

    def shallow_step(c, carry):
        shallow[pl.ds(8 * c + 8, 8)] = (
            grad[pl.ds(8 * c + 8, 8), 8:56, :] * pre_t[pl.ds(8 * c, 8)]
        ).astype(BF16)
        return carry

    lax.fori_loop(0, 6, shallow_step, 0)
    blank = jnp.zeros((64, 122), F32)
    inner = [
        jnp.concatenate([in_w[3 * a + b].astype(F32) for b in range(3)] + [blank], axis=1).astype(BF16)
        for a in range(3)
    ]
    for c in range(7):
        total = jnp.zeros((384, 128), F32)
        for a in range(3):
            total += dot(shallow[8 * c + 8 - 4 * a : 8 * c + 16 - 4 * a].reshape(384, 64), inner[a])
        bands_t[:, 384 * c : 384 * c + 384] = total.T[0:8]
    taps = bands_t[...]
    centre, left, right = taps[2:4], taps[0:2], taps[4:6]
    position = iota((2, 2688), 1)
    line = jnp.zeros((2, 2688), jnp.int32)
    for i in range(1, 56):
        line += jnp.where(position >= 48 * i, 1, 0)
    at = position - 48 * line
    whole = (
        centre
        + jnp.where(at < 44, pltpu.roll(left, 2684, 1), 0.0)
        + jnp.where(at >= 4, pltpu.roll(right, 4, 1), 0.0)
    )
    inside = taps[:, 192:2496].astype(BF16).astype(F32)
    stacked = jnp.concatenate([inside[:, 384 * c : 384 * c + 384] for c in range(6)], axis=0)
    lane, cell8 = iota((384, 128), 1), iota((384, 128), 0)
    half = lane // 32
    source = ((lane % 32) // 4) * 48 + lane % 4 + 44 * half
    taken = jnp.where((source == cell8) & (lane < 64), 1.0, 0.0).astype(BF16)
    sides = dot(stacked.astype(BF16), taken)
    message = [
        jnp.concatenate([whole[0:1, 0:192], whole[1:2, 0:192]], axis=1),
        jnp.concatenate([whole[0:1, 2496:2688], whole[1:2, 2496:2688]], axis=1),
        jnp.concatenate([sides[8 * c + j : 8 * c + j + 1, 0:32] for j in range(2) for c in range(6)], axis=1),
        jnp.concatenate([sides[8 * c + 4 + j : 8 * c + 5 + j, 32:64] for j in range(2) for c in range(6)], axis=1),
    ]
    message = jnp.concatenate(message, axis=0)
    for j in range(3):
        e_send[j] = message[:, 128 * j : 128 * j + 128].astype(BF16)
        e_recv[me, j] = message[:, 128 * j : 128 * j + 128].astype(BF16)

    def tell(i, carry):
        pltpu.make_async_remote_copy(
            e_send, e_recv.at[me], send_sem.at[6], recv_sem.at[6],
            device_id={"tile": lax.rem(me + i, TILES)}, device_id_type=MESH,
        ).start()
        return carry

    lax.fori_loop(1, TILES, tell, 0)
    own = jnp.zeros((8, 256), jnp.int32) - 1
    for side in range(4):
        own = jnp.where(iota((8, 256), 0) == side, seam[me, side, 0] * 4 + seam[me, side, 1], own)
    chosen = jnp.where(own == iota((8, 256), 1), 1.0, 0.0).astype(BF16)
    active = jnp.where(panel[me] < 6, 1.0, 0.0)
    others = pl.ds(0, TILES - 1)
    pltpu.make_async_copy(e_recv.at[others], e_recv.at[others], recv_sem.at[6]).wait()
    pltpu.make_async_copy(e_recv.at[others], e_recv.at[others], send_sem.at[6]).wait()
    rows_from_pieces(rows, e_recv)
    came = jnp.concatenate([dot(chosen, rows[j].astype(BF16)) for j in range(3)], axis=1)
    arrived = jnp.concatenate(
        [
            jnp.concatenate([came[i : i + 1, 192 * j : 192 * j + 192] for i in range(4)], axis=1)
            for j in range(2)
        ]
        + [jnp.zeros((6, 768), F32)],
        axis=0,
    )
    added = dot(arrived.astype(BF16), place[...])
    out_ref[0, 0] = (whole[:, 192:2496] + added[0:2]) * active


def shards(
    pre_act, cotangent, input_weight, conv_weight, down_weight, level_mix, up_weight, head_weight, seam_list,
    tile_panel,
):
    vmem = pl.BlockSpec(memory_space=pltpu.VMEM)
    smem = pl.BlockSpec(memory_space=pltpu.SMEM)
    pieces = pltpu.VMEM((TILES, 3, 4, 128), BF16)
    return pl.pallas_call(
        kernel,
        out_shape=jax.ShapeDtypeStruct((1, 1, 2, 2304), F32),
        in_specs=[vmem, vmem, vmem, vmem, vmem, smem, vmem, vmem, smem, vmem, smem],
        out_specs=vmem,
        scratch_shapes=[
            pltpu.VMEM((48, 48, 64), F32),
            pltpu.VMEM((64, 64, 64), F32),
            pltpu.VMEM((64, 48, 192), BF16),
            pltpu.VMEM((6, 384, 64), BF16),
            pltpu.VMEM((6, 384, 64), F32),
            pltpu.VMEM((6, 384, 64), F32),
            pltpu.VMEM((80, 64, 192), BF16),
            pltpu.VMEM((64, 64, 64), F32),
            pltpu.VMEM((64, 48, 64), BF16),
            pltpu.VMEM((8, 2688), F32),
            pltpu.VMEM((2, 4, 384, 384), BF16),
            pltpu.VMEM((768, 2304), BF16),
            pltpu.VMEM((3, 256, 128), F32),
            pltpu.VMEM((256, 3), jnp.int32),
            pltpu.VMEM((256, 256), BF16),
        ]
        + [pieces] * 8
        + [
            pltpu.VMEM((3, 4, 128), BF16),
            pieces,
            pltpu.VMEM((LEVS, 6, 8, 384), BF16),
            pltpu.VMEM((LEVS, 6, 8, 384), BF16),
            pltpu.SemaphoreType.DMA((7,)),
            pltpu.SemaphoreType.DMA((7,)),
        ],
        compiler_params=pltpu.CompilerParams(
            collective_id=0, has_side_effects=True, vmem_limit_bytes=48 * 2**20
        ),
        name="adjoint",
    )(
        pre_act, cotangent.reshape(6, 1, 384), input_weight, conv_weight, down_weight, level_mix, up_weight,
        head_weight.reshape(1, 64), seam_list, seam_list, tile_panel,
    )


def solution(mesh):
    return jax.shard_map(
        shards,
        mesh=mesh,
        in_specs=(P("tile", "lev", None, None), P("tile", "lev", None), P(), P(), P(), P(), P(), P(), P(), P()),
        out_specs=P("tile", "lev", None, None),
        check_vma=False,
    )
```

time: 281 us -> 126 us (0.45); the launches traced: 276 us -> 126 us
  Pallas kernels: 0 us -> 122 us
  waiting for transfers between devices: 92.6 us -> 0 us
  blocking collectives: 82.2 us -> 0 us
  local copies, waits for them, and re-layouts: 48 us -> 4.06 us
  starting transfers between devices: 37 us -> 0 us
  other arithmetic: 8.04 us -> 0 us
  matrix products: 5.98 us -> 0 us
    pallas_call x0 -> x1, Pallas kernels: none -> 122 us  [shards(): pl.pallas_call(kernel, out_shape=jax.ShapeDtypeStruct((1, 1, 2, 2304), F3...]
    all_to_all x5 -> x0, waiting for transfers between devices: 92.6 us -> none  [the longest x3 56.1 us: route_strips(): lax.all_to_all(picked, 'tile', split_axis=0, concat_axis=1, tiled=True)]
    all_gather x2 -> x0, blocking collectives: 44.7 us -> none  [mix_levels(): lax.all_gather(latents[None], 'lev', axis=0, tiled=True).astype(jnp.float32)]
    all_to_all x1 -> x0, blocking collectives: 37.5 us -> none  [route_strips(): lax.all_to_all(flattened, 'tile', split_axis=1, concat_axis=0, tiled=True)]
    all_to_all x5 -> x0, starting transfers between devices: 37 us -> none  [the longest x2 23.8 us: route_strips(): lax.all_to_all(flattened, 'tile', split_axis=1, concat_axis=0, tiled=True)]
    rev x15 -> x0, local copies, waits for them, and re-layouts: 8.38 us -> none  [the longest x2 3.72 us: add_edges(): jnp.flip(borders[3], axis=1)]
    reshape x11 -> x0, local copies, waits for them, and re-layouts: 7.36 us -> none  [the longest x3 3 us: conv_forward(): padded.reshape(channels, extent * extent)]
    dot_general x18 -> x0, matrix products: 5.98 us -> none  [the longest x12 4.12 us: conv_forward(): jnp.dot(weight_mat, stacked, preferred_element_type=jnp.float32)]
  transfers between devices with their start and end apart: 5 -> 0, of which waited for: 5 -> 0; matrix products, arithmetic and copies ran while one was open for 1% -> 0% of each run, Pallas kernels for 0% -> 0%
where the time goes in v1:
time: 126 us
  Pallas kernels  122 us (97%)
  local copies, waits for them, and re-layouts  4.06 us (3%)
    pallas_call x1, Pallas kernels, shards(): pl.pallas_call(kernel, out_shape=jax.ShapeDtypeStruct((1, 1, 2, 2304), F3...  122 us
    unnamed x18, local copies, waits for them, and re-layouts  4.06 us

profile of v1, /device:TPU:1, one launch (start us, length us, event | category | flops | bytes accessed | tf_op | source)
XLA Modules:
  0.0 125.9 jit_solution(14624659886544619446)
XLA Ops:
  0.0 0.0 copy-start
  0.0 0.8 copy.12.up_ref
  0.8 0.8 copy.13.seam.seam_v
  1.6 0.0 copy-start.2
  1.7 0.0 copy-start.3
  1.7 0.0 copy-start.4
  1.7 0.0 copy-start.5
  1.7 0.0 copy-start.6
  1.7 0.9 copy.11.in_w
  2.6 0.0 copy-done
  2.6 0.0 copy-done.2
  2.6 0.0 copy-done.3
  2.6 0.0 copy-done.4
  2.6 0.0 copy-done.5
  2.6 0.0 copy-done.6
  2.6 0.0 copy-start.1
  2.6 0.9 copy-done.1
  3.5 121.8 %adjoint.1 = f32[1,1,2,2304]{3,2,1,0:T(2,128)S(1)} custom-call(bf16[1,1,64,2304]{3,2,1,0:T(8,128)(2,1)S(1)} %copy-done, bf16[6,1,384]{2,1,0:T(2,128)(2,1)S(1)} %bitcast.2, bf16[9,64,2]{2,1,0:T(8,128)(2,1)S(1)} %copy.11.in_w, bf16[9,64,64]{2,1,0:T(8,128)(2,1)S(1)} %copy-done.1, bf16[8,64]{1,0:T(8,128)(2,1)S(1)} %copy-done.4, f32[8,8]{1,0:T(8,128)S(1)} %copy-done.3, ...), custom_call_target="tpu_custom_call" | custom-call | tf_op jit(solution)/shard_map/adjoint/pallas_call | solution.py:430
  125.3 0.6 copy.16
Async XLA Ops:
  0.0 2.6 %copy-start = (bf16[1,1,64,2304]{3,2,1,0:T(8,128)(2,1)S(1)}, bf16[1,1,64,2304]{3,2,1,0:T(8,128)(2,1)}, u32[]{:S(2)}) copy-start(bf16[1,1,64,2304]{3,2,1,0:T(8,128)(2,1)} %pre_ref.1) | copy-start | bytes 884740
  1.6 0.9 copy-start.2
  1.7 0.9 copy-start.3
  1.7 0.9 copy-start.4
  1.7 0.9 copy-start.5
  1.7 0.9 copy-start.6
  2.6 0.9 copy-start.1

commit v2 on v1

--- a/solution.py
+++ b/solution.py
@@ -29,34 +29,38 @@
     return lax.broadcasted_iota(jnp.int32, shape, axis)
 
 
-def rows_from_pieces(rows, pieces):
+def peer_at(me, i):
+    back = TILES - i
+    half = (back + 1) // 2
+    return jnp.bitwise_and(me + jnp.where(lax.rem(back, 2) == 1, half, TILES - half), TILES - 1)
+
+
+def rows_from_pieces(rows, j, pieces):
     view = rows.reshape(3, 32, 8, 128)
 
     def step(m, carry):
-        for h in range(2):
-            for j in range(3):
-                view[j, m, 4 * h : 4 * h + 4, :] = pieces[2 * m + h, j].astype(F32)
-        return carry
-
-    lax.fori_loop(0, 32, step, 0)
-
-
-def pieces_from_rows(pieces, rows):
+        for k in range(4):
+            for h in range(2):
+                view[j, 4 * m + k, 4 * h : 4 * h + 4, :] = pieces[8 * m + 2 * k + h].astype(F32)
+        return carry
+
+    lax.fori_loop(0, 8, step, 0)
+
+
+def pieces_from_rows(pieces, rows, j):
     view = rows.reshape(3, 32, 8, 128)
 
     def step(m, carry):
-        for h in range(2):
-            for j in range(3):
-                pieces[2 * m + h, j] = view[j, m, 4 * h : 4 * h + 4, :].astype(BF16)
-        return carry
-
-    lax.fori_loop(0, 32, step, 0)
-
-
-def rows_from_slab(rows, member, slab):
-    for j in range(3):
-        block = jnp.concatenate([slab[128 * j : 128 * j + 64], slab[128 * j + 64 : 128 * j + 128]], axis=1)
-        rows[j, pl.ds(member, 64, stride=4), :] = block
+        for k in range(4):
+            for h in range(2):
+                pieces[8 * m + 2 * k + h] = view[j, 4 * m + k, 4 * h : 4 * h + 4, :].astype(BF16)
+        return carry
+
+    lax.fori_loop(0, 8, step, 0)
+
+
+def slab_to_rows(rows, j, member, slab):
+    rows[j, pl.ds(member, 64, stride=4), :] = jnp.concatenate([slab[0:64], slab[64:128]], axis=1)
 
 
 def slab_from_rows(rows, member):
@@ -67,13 +71,13 @@
     return jnp.concatenate(parts, axis=0)
 
 
-def spread_start(send, recv, send_sem, recv_sem, me):
+def spread_start(send, recv, sems, me):
     recv[me] = send[me]
 
     def step(i, carry):
-        target = lax.rem(me + i, TILES)
+        target = peer_at(me, i)
         pltpu.make_async_remote_copy(
-            send.at[target], recv.at[me], send_sem, recv_sem,
+            send.at[target], recv.at[me], sems.at[0], sems.at[1],
             device_id={"tile": target}, device_id_type=MESH,
         ).start()
         return carry
@@ -81,29 +85,41 @@
     lax.fori_loop(1, TILES, step, 0)
 
 
-def spread_wait(send, recv, send_sem, recv_sem):
-    others = pl.ds(0, TILES - 1)
-    pltpu.make_async_copy(recv.at[others], recv.at[others], recv_sem).wait()
-    pltpu.make_async_copy(send.at[others], send.at[others], send_sem).wait()
-
-
-def level_start(buf, send_sem, recv_sem, level):
-    for i in range(1, LEVS):
+def arrived_all(ref, count, sem):
+    some = ref.at[pl.ds(0, count)]
+    pltpu.make_async_copy(some, some, sem).wait()
+
+
+def strips_out(slabs, rows, send, recv, sems, me):
+    for j in range(3):
+        for member in range(4):
+            slab_to_rows(rows, j, member, slabs[member](j))
+        pieces_from_rows(send.at[j], rows, j)
+        spread_start(send.at[j], recv.at[j], sems.at[j], me)
+
+
+def strips_on(choice, rows, first_recv, first_sems, send, recv, sems, me):
+    for j in range(3):
+        arrived_all(first_recv.at[j], TILES - 1, first_sems.at[j, 1])
+        rows_from_pieces(rows, j, first_recv.at[j])
+        rows[j] = dot(choice[...], rows[j].astype(BF16))
+        pieces_from_rows(send.at[j], rows, j)
+        spread_start(send.at[j], recv.at[j], sems.at[j], me)
+
+
+def strips_in(turns, rows, recv, sems):
+    for j in range(3):
+        arrived_all(recv.at[j], TILES - 1, sems.at[j, 1])
+        rows_from_pieces(rows, j, recv.at[j])
+    return [dot(turns[side], slab_from_rows(rows, side).astype(BF16)) for side in range(4)]
+
+
+def level_start(buf, c, sems, level):
+    for i in (4, 3, 5, 2, 6, 1, 7):
         pltpu.make_async_remote_copy(
-            buf.at[level], buf.at[level], send_sem, recv_sem,
-            device_id={"lev": lax.rem(level + i, LEVS)}, device_id_type=MESH,
+            buf.at[c, level], buf.at[c, level], sems.at[c, 0], sems.at[c, 1],
+            device_id={"lev": jnp.bitwise_and(level + i, LEVS - 1)}, device_id_type=MESH,
         ).start()
-
-
-def level_wait(buf, send_sem, recv_sem):
-    others = pl.ds(0, LEVS - 1)
-    pltpu.make_async_copy(buf.at[others], buf.at[others], recv_sem).wait()
-    pltpu.make_async_copy(buf.at[others], buf.at[others], send_sem).wait()
-
-
-def pick(rows, choice):
-    for j in range(3):
-        rows[j] = dot(choice, rows[j].astype(BF16))
 
 
 def turn_matrix(side, edge, flip, of_bands):
@@ -129,15 +145,15 @@
 def kernel(
     pre_ref, cot_ref, in_w, conv_w, down_ref, mix_ref, up_ref, head_ref, seam, seam_v, panel, out_ref,
     pre_t, padded, wide, act, second, top, deep_wide, grad, shallow, bands_t, turns, place, rows, wanted,
-    choice, a_send, a_recv, b_send, b_recv, c_send, c_recv, d_send, d_recv, e_send, e_recv, lat, glat,
-    send_sem, recv_sem,
+    choice, a_send, a_recv, b_send, b_recv, c_send, c_recv, d_send, d_recv, e_send, e_recv, f_send, f_recv, lat, glat,
+    tile_sems, lat_sems, glat_sems, last_sems,
 ):
     me = lax.axis_index("tile")
     level = lax.axis_index("lev")
     barrier = pltpu.get_barrier_semaphore()
 
     def greet(i, carry):
-        pl.semaphore_signal(barrier, inc=1, device_id={"tile": lax.rem(me + i, TILES)}, device_id_type=MESH)
+        pl.semaphore_signal(barrier, inc=1, device_id={"tile": peer_at(me, i)}, device_id_type=MESH)
         return carry
 
     lax.fori_loop(1, TILES, greet, 0)
@@ -155,13 +171,20 @@
         return carry
 
     lax.fori_loop(0, 6, first, 0)
-    rows_from_slab(rows, 0, padded[8:16, 8:56, :].reshape(384, 64))
-    rows_from_slab(rows, 1, padded[48:56, 8:56, :].reshape(384, 64))
-    rows_from_slab(rows, 2, padded[8:56, 8:16, :].reshape(384, 64))
-    rows_from_slab(rows, 3, padded[8:56, 48:56, :].reshape(384, 64))
-    pieces_from_rows(a_send, rows)
     pl.semaphore_wait(barrier, TILES - 1 + LEVS - 1)
-    spread_start(a_send, a_recv, send_sem.at[0], recv_sem.at[0], me)
+
+    def edges_of(ref, places):
+        def rows_at(r, c0):
+            return lambda j: ref[r : r + 8, c0 : c0 + 48, :].reshape(384, 64)[128 * j : 128 * j + 128]
+
+        def columns_at(r, c0):
+            return lambda j: ref[r + 16 * j : r + 16 * j + 16, c0 : c0 + 8, :].reshape(128, 64)
+
+        return [rows_at(*places[0]), rows_at(*places[1]), columns_at(*places[2]), columns_at(*places[3])]
+
+    strips_out(
+        edges_of(padded, [(8, 8), (48, 8), (8, 8), (8, 48)]), rows, a_send, a_recv, tile_sems.at[0], me
+    )
 
     wide_view = wanted.reshape(32, 8, 3)
 
@@ -180,18 +203,12 @@
     for side in range(4):
         turns[0, side] = turn_matrix(side, seam[me, side, 1], seam[me, side, 2], False)
 
-    spread_wait(a_send, a_recv, send_sem.at[0], recv_sem.at[0])
-    rows_from_pieces(rows, a_recv)
-    pick(rows, choice[...])
-    pieces_from_rows(b_send, rows)
-    spread_start(b_send, b_recv, send_sem.at[1], recv_sem.at[1], me)
+    strips_on(choice, rows, a_recv, tile_sems.at[0], b_send, b_recv, tile_sems.at[1], me)
 
     for side in range(4):
         turns[1, side] = turn_matrix(side, seam[me, side, 1], seam[me, side, 2], True)
 
-    spread_wait(b_send, b_recv, send_sem.at[1], recv_sem.at[1])
-    rows_from_pieces(rows, b_recv)
-    rims = [dot(turns[0, side], slab_from_rows(rows, side).astype(BF16)) for side in range(4)]
+    rims = strips_in(turns.at[0], rows, b_recv, tile_sems.at[1])
     padded[0:8, 8:56, :] = rims[0].reshape(8, 48, 64)
     padded[56:64, 8:56, :] = rims[1].reshape(8, 48, 64)
     padded[8:56, 0:8, :] = rims[2].reshape(48, 8, 64)
@@ -216,11 +233,11 @@
         second[c] = total
         s = (total * jax.nn.sigmoid(total)).astype(BF16)
         act[c] = s
-        lat[level, c] = dot(down, s, NT).astype(BF16)
+        lat[c, level] = dot(down, s, NT).astype(BF16)
+        level_start(lat, c, lat_sems, level)
         return carry
 
     lax.fori_loop(0, 6, conv, 0)
-    level_start(lat, send_sem.at[2], recv_sem.at[2], level)
 
     head = head_ref[...]
     high = head.astype(BF16)
@@ -234,37 +251,37 @@
     eye = jnp.where(iota((8, 8), 0) == iota((8, 8), 1), 1.0, 0.0).astype(BF16)
     up_t = dot(eye, up, NT).astype(BF16)
 
-    level_wait(lat, send_sem.at[2], recv_sem.at[2])
+    def clear(c, carry):
+        deep_wide[pl.ds(8 * c, 8)] = jnp.zeros((8, 64, 192), BF16)
+        deep_wide[pl.ds(64 + 8 * c, 8)] = jnp.zeros((8, 64, 192), BF16)
+        return carry
+
+    lax.fori_loop(0, 2, clear, 0)
+    shallow[0:8] = jnp.zeros((8, 48, 64), BF16)
+    shallow[56:64] = jnp.zeros((8, 48, 64), BF16)
 
     def top_step(c, carry):
-        mixed = mix_ref[level, 0] * lat[0, c].astype(F32)
+        arrived_all(lat.at[c], LEVS - 1, lat_sems.at[c, 1])
+        mixed = mix_ref[level, 0] * lat[c, 0].astype(F32)
         for other in range(1, LEVS):
-            mixed += mix_ref[level, other] * lat[other, c].astype(F32)
+            mixed += mix_ref[level, other] * lat[c, other].astype(F32)
         mixed = mixed.astype(BF16).astype(F32).T.astype(BF16)
         third = act[c].astype(F32) + dot(mixed, up, NT)
         cot = jnp.broadcast_to(cot_ref[c].astype(F32), (8, 384)).T.astype(BF16)
         gradient = dot(cot, heads) * dsilu(third)
         top[c] = gradient
-        glat[level, c] = dot(up_t, gradient.astype(BF16), NT).astype(BF16)
-        return carry
+        glat[c, level] = dot(up_t, gradient.astype(BF16), NT).astype(BF16)
+        level_start(glat, c, glat_sems, level)
+        return carry
+
 
     lax.fori_loop(0, 6, top_step, 0)
-    level_start(glat, send_sem.at[3], recv_sem.at[3], level)
-
-    def clear(c, carry):
-        deep_wide[pl.ds(8 * c, 8)] = jnp.zeros((8, 64, 192), BF16)
-        deep_wide[pl.ds(64 + 8 * c, 8)] = jnp.zeros((8, 64, 192), BF16)
-        return carry
-
-    lax.fori_loop(0, 2, clear, 0)
-    shallow[0:8] = jnp.zeros((8, 48, 64), BF16)
-    shallow[56:64] = jnp.zeros((8, 48, 64), BF16)
-    level_wait(glat, send_sem.at[3], recv_sem.at[3])
 
     def deep_step(c, carry):
-        mixed = mix_ref[0, level] * glat[0, c].astype(F32)
+        arrived_all(glat.at[c], LEVS - 1, glat_sems.at[c, 1])
+        mixed = mix_ref[0, level] * glat[c, 0].astype(F32)
         for other in range(1, LEVS):
-            mixed += mix_ref[other, level] * glat[other, c].astype(F32)
+            mixed += mix_ref[other, level] * glat[c, other].astype(F32)
         mixed = mixed.astype(BF16).astype(F32).T.astype(BF16)
         gradient = top[c] + dot(mixed, down)
         d = (gradient * dsilu(second[c])).reshape(8, 48, 64)
@@ -292,12 +309,9 @@
         return carry
 
     lax.fori_loop(0, 8, adjoint, 0)
-    rows_from_slab(rows, 0, grad[0:8, 8:56, :].reshape(384, 64))
-    rows_from_slab(rows, 1, grad[56:64, 8:56, :].reshape(384, 64))
-    rows_from_slab(rows, 2, grad[8:56, 0:8, :].reshape(384, 64))
-    rows_from_slab(rows, 3, grad[8:56, 56:64, :].reshape(384, 64))
-    pieces_from_rows(c_send, rows)
-    spread_start(c_send, c_recv, send_sem.at[4], recv_sem.at[4], me)
+    strips_out(
+        edges_of(grad, [(0, 8), (56, 8), (8, 0), (8, 56)]), rows, c_send, c_recv, tile_sems.at[2], me
+    )
 
     def slope(c, carry):
         pre_t[pl.ds(8 * c, 8)] = dsilu(pre_t[pl.ds(8 * c, 8)])
@@ -330,14 +344,8 @@
 
         lax.fori_loop(0, 12, put, 0)
 
-    spread_wait(c_send, c_recv, send_sem.at[4], recv_sem.at[4])
-    rows_from_pieces(rows, c_recv)
-    pick(rows, choice[...])
-    pieces_from_rows(d_send, rows)
-    spread_start(d_send, d_recv, send_sem.at[5], recv_sem.at[5], me)
-    spread_wait(d_send, d_recv, send_sem.at[5], recv_sem.at[5])
-    rows_from_pieces(rows, d_recv)
-    rims = [dot(turns[1, side], slab_from_rows(rows, side).astype(BF16)) for side in range(4)]
+    strips_on(choice, rows, c_recv, tile_sems.at[2], d_send, d_recv, tile_sems.at[3], me)
+    rims = strips_in(turns.at[1], rows, d_recv, tile_sems.at[3])
     grad[8:16, 8:56, :] += rims[0].reshape(8, 48, 64)
     grad[48:56, 8:56, :] += rims[1].reshape(8, 48, 64)
     grad[8:56, 8:16, :] += rims[2].reshape(48, 8, 64)
@@ -386,28 +394,55 @@
         jnp.concatenate([sides[8 * c + 4 + j : 8 * c + 5 + j, 32:64] for j in range(2) for c in range(6)], axis=1),
     ]
     message = jnp.concatenate(message, axis=0)
+    depth, quarter = me // 4, lax.rem(me, 4)
     for j in range(3):
         e_send[j] = message[:, 128 * j : 128 * j + 128].astype(BF16)
-        e_recv[me, j] = message[:, 128 * j : 128 * j + 128].astype(BF16)
+        e_recv[depth, j] = message[:, 128 * j : 128 * j + 128].astype(BF16)
 
     def tell(i, carry):
+        back = 16 - i
+        half = (back + 1) // 2
+        there = jnp.bitwise_and(depth + jnp.where(lax.rem(back, 2) == 1, half, 16 - half), 15)
         pltpu.make_async_remote_copy(
-            e_send, e_recv.at[me], send_sem.at[6], recv_sem.at[6],
-            device_id={"tile": lax.rem(me + i, TILES)}, device_id_type=MESH,
+            e_send, e_recv.at[depth], last_sems.at[0, 0], last_sems.at[0, 1],
+            device_id={"tile": 4 * there + quarter}, device_id_type=MESH,
         ).start()
         return carry
 
-    lax.fori_loop(1, TILES, tell, 0)
-    own = jnp.zeros((8, 256), jnp.int32) - 1
-    for side in range(4):
-        own = jnp.where(iota((8, 256), 0) == side, seam[me, side, 0] * 4 + seam[me, side, 1], own)
-    chosen = jnp.where(own == iota((8, 256), 1), 1.0, 0.0).astype(BF16)
+    lax.fori_loop(1, 16, tell, 0)
+    row_of = iota((16, 64), 0)
+    own = jnp.zeros((16, 64), jnp.int32) - 1
+    for member in range(4):
+        for side in range(4):
+            peer = seam[4 * depth + member, side, 0]
+            held = jnp.where(lax.rem(peer, 4) == quarter, (peer // 4) * 4 + seam[4 * depth + member, side, 1], -1)
+            own = jnp.where(row_of == 4 * member + side, held, own)
+    chosen = jnp.where(own == iota((16, 64), 1), 1.0, 0.0).astype(BF16)
     active = jnp.where(panel[me] < 6, 1.0, 0.0)
-    others = pl.ds(0, TILES - 1)
-    pltpu.make_async_copy(e_recv.at[others], e_recv.at[others], recv_sem.at[6]).wait()
-    pltpu.make_async_copy(e_recv.at[others], e_recv.at[others], send_sem.at[6]).wait()
-    rows_from_pieces(rows, e_recv)
-    came = jnp.concatenate([dot(chosen, rows[j].astype(BF16)) for j in range(3)], axis=1)
+    arrived_all(e_recv, 15, last_sems.at[0, 1])
+    for j in range(3):
+        view = rows.reshape(3, 32, 8, 128)
+        for m in range(8):
+            for h in range(2):
+                view[j, m, 4 * h : 4 * h + 4, :] = e_recv[2 * m + h, j].astype(F32)
+        found = dot(chosen, rows[j, 0:64].astype(BF16))
+        for member in range(4):
+            f_send[member, j] = found[4 * member : 4 * member + 4].astype(BF16)
+    f_recv[quarter] = f_send[quarter]
+    for i in (3, 2, 1):
+        there = jnp.bitwise_xor(quarter, i)
+        pltpu.make_async_remote_copy(
+            f_send.at[there], f_recv.at[quarter], last_sems.at[1, 0], last_sems.at[1, 1],
+            device_id={"tile": 4 * depth + there}, device_id_type=MESH,
+        ).start()
+    arrived_all(f_recv, 3, last_sems.at[1, 1])
+    came = []
+    for j in range(3):
+        part = f_recv[0, j].astype(F32)
+        for member in range(1, 4):
+            part += f_recv[member, j].astype(F32)
+        came.append(part)
+    came = jnp.concatenate(came, axis=1)
     arrived = jnp.concatenate(
         [
             jnp.concatenate([came[i : i + 1, 192 * j : 192 * j + 192] for i in range(4)], axis=1)
@@ -418,6 +453,14 @@
     )
     added = dot(arrived.astype(BF16), place[...])
     out_ref[0, 0] = (whole[:, 192:2496] + added[0:2]) * active
+    for phase, buf in enumerate((a_send, b_send, c_send, d_send)):
+        for j in range(3):
+            arrived_all(buf.at[j], TILES - 1, tile_sems.at[phase, j, 0])
+    for c in range(6):
+        arrived_all(lat.at[c], LEVS - 1, lat_sems.at[c, 0])
+        arrived_all(glat.at[c], LEVS - 1, glat_sems.at[c, 0])
+    arrived_all(e_recv, 15, last_sems.at[0, 0])
+    arrived_all(f_send, 3, last_sems.at[1, 0])
 
 
 def shards(
@@ -426,7 +469,7 @@
 ):
     vmem = pl.BlockSpec(memory_space=pltpu.VMEM)
     smem = pl.BlockSpec(memory_space=pltpu.SMEM)
-    pieces = pltpu.VMEM((TILES, 3, 4, 128), BF16)
+    pieces = pltpu.VMEM((3, TILES, 4, 128), BF16)
     return pl.pallas_call(
         kernel,
         out_shape=jax.ShapeDtypeStruct((1, 1, 2, 2304), F32),
@@ -452,11 +495,15 @@
         + [pieces] * 8
         + [
             pltpu.VMEM((3, 4, 128), BF16),
-            pieces,
-            pltpu.VMEM((LEVS, 6, 8, 384), BF16),
-            pltpu.VMEM((LEVS, 6, 8, 384), BF16),
-            pltpu.SemaphoreType.DMA((7,)),
-            pltpu.SemaphoreType.DMA((7,)),
+            pltpu.VMEM((16, 3, 4, 128), BF16),
+            pltpu.VMEM((4, 3, 4, 128), BF16),
+            pltpu.VMEM((4, 3, 4, 128), BF16),
+            pltpu.VMEM((6, LEVS, 8, 384), BF16),
+            pltpu.VMEM((6, LEVS, 8, 384), BF16),
+            pltpu.SemaphoreType.DMA((4, 3, 2)),
+            pltpu.SemaphoreType.DMA((6, 2)),
+            pltpu.SemaphoreType.DMA((6, 2)),
+            pltpu.SemaphoreType.DMA((2, 2)),
         ],
         compiler_params=pltpu.CompilerParams(
             collective_id=0, has_side_effects=True, vmem_limit_bytes=48 * 2**20

time: 126 us -> 102 us (0.81)
  Pallas kernels: 122 us -> 97.6 us
    pallas_call x1, Pallas kernels: 122 us -> 97.6 us  [shards(): pl.pallas_call(kernel, out_shape=jax.ShapeDtypeStruct((1, 1, 2, 2304), F3...]
where the time goes in v2:
time: 102 us
  Pallas kernels  97.6 us (96%)
  local copies, waits for them, and re-layouts  4.06 us (4%)
    pallas_call x1, Pallas kernels, shards(): pl.pallas_call(kernel, out_shape=jax.ShapeDtypeStruct((1, 1, 2, 2304), F3...  97.6 us
    unnamed x18, local copies, waits for them, and re-layouts  4.06 us

profile of v2, /device:TPU:1, one launch (start us, length us, event | category | flops | bytes accessed | tf_op | source)
XLA Modules:
  0.0 101.7 jit_solution(4116950401641006500)
XLA Ops:
  0.0 0.0 copy-start
  0.0 0.8 copy.12.up_ref
  0.8 0.8 copy.13.seam.seam_v
  1.6 0.0 copy-start.2
  1.7 0.0 copy-start.3
  1.7 0.0 copy-start.4
  1.7 0.0 copy-start.5
  1.7 0.0 copy-start.6
  1.7 0.9 copy.11.in_w
  2.6 0.0 copy-done
  2.6 0.0 copy-done.2
  2.6 0.0 copy-done.3
  2.6 0.0 copy-done.4
  2.6 0.0 copy-done.5
  2.6 0.0 copy-done.6
  2.6 0.0 copy-start.1
  2.6 0.9 copy-done.1
  3.5 97.6 %adjoint.1 = f32[1,1,2,2304]{3,2,1,0:T(2,128)S(1)} custom-call(bf16[1,1,64,2304]{3,2,1,0:T(8,128)(2,1)S(1)} %copy-done, bf16[6,1,384]{2,1,0:T(2,128)(2,1)S(1)} %bitcast.2, bf16[9,64,2]{2,1,0:T(8,128)(2,1)S(1)} %copy.11.in_w, bf16[9,64,64]{2,1,0:T(8,128)(2,1)S(1)} %copy-done.1, bf16[8,64]{1,0:T(8,128)(2,1)S(1)} %copy-done.4, f32[8,8]{1,0:T(8,128)S(1)} %copy-done.3, ...), custom_call_target="tpu_custom_call" | custom-call | tf_op jit(solution)/shard_map/adjoint/pallas_call | solution.py:473
  101.1 0.6 copy.16
Async XLA Ops:
  0.0 2.6 %copy-start = (bf16[1,1,64,2304]{3,2,1,0:T(8,128)(2,1)S(1)}, bf16[1,1,64,2304]{3,2,1,0:T(8,128)(2,1)}, u32[]{:S(2)}) copy-start(bf16[1,1,64,2304]{3,2,1,0:T(8,128)(2,1)} %pre_ref.1) | copy-start | bytes 884740
  1.6 0.9 copy-start.2
  1.7 0.9 copy-start.3
  1.7 0.9 copy-start.4
  1.7 0.9 copy-start.5
  1.7 0.9 copy-start.6
  2.6 0.9 copy-start.1

commit v3 on v2

--- a/solution.py
+++ b/solution.py
@@ -143,13 +143,17 @@
 
 
 def kernel(
-    pre_ref, cot_ref, in_w, conv_w, down_ref, mix_ref, up_ref, head_ref, seam, seam_v, panel, out_ref,
+    pre_hbm, cot_ref, in_w, conv_hbm, down_ref, mix_ref, up_ref, head_ref, seam, seam_v, panel, out_ref,
     pre_t, padded, wide, act, second, top, deep_wide, grad, shallow, bands_t, turns, place, rows, wanted,
     choice, a_send, a_recv, b_send, b_recv, c_send, c_recv, d_send, d_recv, e_send, e_recv, f_send, f_recv, lat, glat,
-    tile_sems, lat_sems, glat_sems, last_sems,
+    tile_sems, lat_sems, glat_sems, last_sems, pre_ref, conv_w, load_sems,
 ):
     me = lax.axis_index("tile")
     level = lax.axis_index("lev")
+    load_pre = pltpu.make_async_copy(pre_hbm, pre_ref, load_sems.at[0])
+    load_pre.start()
+    load_conv = pltpu.make_async_copy(conv_hbm, conv_w, load_sems.at[1])
+    load_conv.start()
     barrier = pltpu.get_barrier_semaphore()
 
     def greet(i, carry):
@@ -160,9 +164,10 @@
     for i in range(1, LEVS):
         pl.semaphore_signal(barrier, inc=1, device_id={"lev": lax.rem(level + i, LEVS)}, device_id_type=MESH)
 
+    load_pre.wait()
     pre_t[...] = pre_ref[0, 0].astype(F32).T.reshape(48, 48, 64)
-    padded[0:8] = jnp.zeros((8, 64, 64), F32)
-    padded[56:64] = jnp.zeros((8, 64, 64), F32)
+    padded[8:56, 0:8, :] = jnp.zeros((48, 8, 64), F32)
+    padded[8:56, 56:64, :] = jnp.zeros((48, 8, 64), F32)
 
     def first(c, carry):
         v = pre_t[pl.ds(8 * c, 8)]
@@ -186,42 +191,31 @@
         edges_of(padded, [(8, 8), (48, 8), (8, 8), (8, 48)]), rows, a_send, a_recv, tile_sems.at[0], me
     )
 
-    wide_view = wanted.reshape(32, 8, 3)
-
-    def want(m, carry):
-        for h in range(2):
-            wide_view[m, 4 * h : 4 * h + 4, :] = seam_v[2 * m + h]
-        return carry
-
-    lax.fori_loop(0, 32, want, 0)
+    wished = (seam_v[0] * 4 + seam_v[1]).astype(F32)
+    wished = jnp.concatenate([wished, jnp.zeros((4, 64), F32)], axis=0)
+    wished = jnp.concatenate([wished, jnp.zeros((8, 64), F32)], axis=1).T
+    for side in range(4):
+        wanted[pl.ds(side, 64, stride=4), :] = jnp.broadcast_to(
+            wished[0:64, side : side + 1], (64, 128)
+        ).astype(jnp.int32)
     table = wanted[...]
-    wished = table[:, 0:1] * 4 + table[:, 1:2]
     for j in range(2):
         choice[:, 128 * j : 128 * j + 128] = jnp.where(
-            wished == iota((256, 128), 1) + 128 * j, 1.0, 0.0
+            table == iota((256, 128), 1) + 128 * j, 1.0, 0.0
         ).astype(BF16)
-    for side in range(4):
-        turns[0, side] = turn_matrix(side, seam[me, side, 1], seam[me, side, 2], False)
-
-    strips_on(choice, rows, a_recv, tile_sems.at[0], b_send, b_recv, tile_sems.at[1], me)
-
-    for side in range(4):
-        turns[1, side] = turn_matrix(side, seam[me, side, 1], seam[me, side, 2], True)
-
-    rims = strips_in(turns.at[0], rows, b_recv, tile_sems.at[1])
-    padded[0:8, 8:56, :] = rims[0].reshape(8, 48, 64)
-    padded[56:64, 8:56, :] = rims[1].reshape(8, 48, 64)
-    padded[8:56, 0:8, :] = rims[2].reshape(48, 8, 64)
-    padded[8:56, 56:64, :] = rims[3].reshape(48, 8, 64)
+
+    load_conv.wait()
+    wide[0:8] = jnp.zeros((8, 48, 192), BF16)
+    wide[56:64] = jnp.zeros((8, 48, 192), BF16)
 
     def widen(c, carry):
         x = padded[pl.ds(8 * c, 8)]
         wide[pl.ds(8 * c, 8)] = jnp.concatenate([x[:, 0:48], x[:, 8:56], x[:, 16:64]], axis=2).astype(BF16)
         return carry
 
-    lax.fori_loop(0, 8, widen, 0)
+    lax.fori_loop(1, 7, widen, 0)
     down = down_ref[...]
-    up = up_ref[...]
+    up_t = up_ref[...]
     forward = [
         jnp.concatenate([conv_w[3 * a + b] for b in range(3)], axis=1) for a in range(3)
     ]
@@ -230,14 +224,15 @@
         total = jnp.zeros((384, 64), F32)
         for a in range(3):
             total += dot(wide[pl.ds(8 * (c + a), 8)].reshape(384, 192), forward[a], NT)
-        second[c] = total
-        s = (total * jax.nn.sigmoid(total)).astype(BF16)
-        act[c] = s
-        lat[c, level] = dot(down, s, NT).astype(BF16)
-        level_start(lat, c, lat_sems, level)
+        second[pl.ds(8 * c, 8)] = total.reshape(8, 48, 64)
         return carry
 
     lax.fori_loop(0, 6, conv, 0)
+
+    strips_on(choice, rows, a_recv, tile_sems.at[0], b_send, b_recv, tile_sems.at[1], me)
+
+    for side in range(4):
+        turns[0, side] = turn_matrix(side, seam[1, side, me], seam[2, side, me], False)
 
     head = head_ref[...]
     high = head.astype(BF16)
@@ -248,8 +243,6 @@
     heads = jnp.concatenate(
         [high.astype(F32), middle.astype(F32), low.astype(F32), zero_rows], axis=0
     ).astype(BF16)
-    eye = jnp.where(iota((8, 8), 0) == iota((8, 8), 1), 1.0, 0.0).astype(BF16)
-    up_t = dot(eye, up, NT).astype(BF16)
 
     def clear(c, carry):
         deep_wide[pl.ds(8 * c, 8)] = jnp.zeros((8, 64, 192), BF16)
@@ -259,6 +252,37 @@
     lax.fori_loop(0, 2, clear, 0)
     shallow[0:8] = jnp.zeros((8, 48, 64), BF16)
     shallow[56:64] = jnp.zeros((8, 48, 64), BF16)
+
+    rims = strips_in(turns.at[0], rows, b_recv, tile_sems.at[1])
+    edge = jnp.zeros((8, 8, 64), F32)
+    for side, a in ((0, 0), (1, 2)):
+        rim = rims[side].reshape(8, 48, 64)
+        shifted = jnp.concatenate(
+            [
+                jnp.concatenate([edge, rim[:, 0:40]], axis=1),
+                rim,
+                jnp.concatenate([rim[:, 8:48], edge], axis=1),
+            ],
+            axis=2,
+        )
+        extra = dot(shifted.reshape(384, 192).astype(BF16), forward[a], NT)
+        second[20 * a : 20 * a + 8] += extra.reshape(8, 48, 64)
+    for side, b in ((2, 0), (3, 2)):
+        rim = jnp.concatenate([edge, rims[side].reshape(48, 8, 64), edge], axis=0)
+        extra = jnp.zeros((384, 64), F32)
+        for a in range(3):
+            extra += dot(rim[8 * a : 8 * a + 48].reshape(384, 64).astype(BF16), conv_w[3 * a + b], NT)
+        second[:, 20 * b : 20 * b + 8, :] += extra.reshape(48, 8, 64)
+
+    def squash(c, carry):
+        total = second[pl.ds(8 * c, 8)].reshape(384, 64)
+        s = (total * jax.nn.sigmoid(total)).astype(BF16)
+        act[c] = s
+        lat[c, level] = dot(down, s, NT).astype(BF16)
+        level_start(lat, c, lat_sems, level)
+        return carry
+
+    lax.fori_loop(0, 6, squash, 0)
 
     def top_step(c, carry):
         arrived_all(lat.at[c], LEVS - 1, lat_sems.at[c, 1])
@@ -266,7 +290,7 @@
         for other in range(1, LEVS):
             mixed += mix_ref[level, other] * lat[c, other].astype(F32)
         mixed = mixed.astype(BF16).astype(F32).T.astype(BF16)
-        third = act[c].astype(F32) + dot(mixed, up, NT)
+        third = act[c].astype(F32) + dot(mixed, up_t)
         cot = jnp.broadcast_to(cot_ref[c].astype(F32), (8, 384)).T.astype(BF16)
         gradient = dot(cot, heads) * dsilu(third)
         top[c] = gradient
@@ -284,7 +308,7 @@
             mixed += mix_ref[other, level] * glat[c, other].astype(F32)
         mixed = mixed.astype(BF16).astype(F32).T.astype(BF16)
         gradient = top[c] + dot(mixed, down)
-        d = (gradient * dsilu(second[c])).reshape(8, 48, 64)
+        d = (gradient * dsilu(second[pl.ds(8 * c, 8)].reshape(384, 64))).reshape(8, 48, 64)
         z8 = jnp.zeros((8, 8, 64), F32)
         z16 = jnp.zeros((8, 16, 64), F32)
         joined = jnp.concatenate(
@@ -301,17 +325,26 @@
     lax.fori_loop(0, 6, deep_step, 0)
     backward = [conv_w[3 * a : 3 * a + 3].reshape(192, 64) for a in range(3)]
 
+    grad[0:8] = dot(deep_wide[16:24].reshape(512, 192), backward[0]).reshape(8, 64, 64)
+    grad[56:64] = dot(deep_wide[56:64].reshape(512, 192), backward[2]).reshape(8, 64, 64)
+    for near, far, take in ((0, 0, 0), (48, 56, 8)):
+        total = jnp.zeros((768, 64), F32)
+        for a in range(3):
+            start = 8 * (3 - a)
+            total += dot(deep_wide[start : start + 48, near : near + 16, :].reshape(768, 192), backward[a])
+        grad[8:56, far : far + 8, :] = total.reshape(48, 16, 64)[:, take : take + 8]
+    strips_out(
+        edges_of(grad, [(0, 8), (56, 8), (8, 0), (8, 56)]), rows, c_send, c_recv, tile_sems.at[2], me
+    )
+
     def adjoint(c, carry):
         total = jnp.zeros((512, 64), F32)
         for a in range(3):
             total += dot(deep_wide[pl.ds(8 * (c + 2 - a), 8)].reshape(512, 192), backward[a])
-        grad[pl.ds(8 * c, 8)] = total.reshape(8, 64, 64)
-        return carry
-
-    lax.fori_loop(0, 8, adjoint, 0)
-    strips_out(
-        edges_of(grad, [(0, 8), (56, 8), (8, 0), (8, 56)]), rows, c_send, c_recv, tile_sems.at[2], me
-    )
+        grad[pl.ds(8 * c, 8), 8:56, :] = total.reshape(8, 64, 64)[:, 8:56]
+        return carry
+
+    lax.fori_loop(1, 7, adjoint, 0)
 
     def slope(c, carry):
         pre_t[pl.ds(8 * c, 8)] = dsilu(pre_t[pl.ds(8 * c, 8)])
@@ -324,7 +357,7 @@
         row += jnp.where(cell >= 48 * i, 1, 0)
     column = cell - 48 * row
     for side in range(4):
-        edge, flip = seam[me, side, 1], seam[me, side, 2]
+        edge, flip = seam[1, side, me], seam[2, side, me]
         a, b = [(row, column), (47 - row, column), (column, row), (47 - column, row)][side]
         turned = 1 - lax.rem(edge, 2)
         by_rows = jnp.where(edge < 2, 1, 0)
@@ -345,6 +378,8 @@
         lax.fori_loop(0, 12, put, 0)
 
     strips_on(choice, rows, c_recv, tile_sems.at[2], d_send, d_recv, tile_sems.at[3], me)
+    for side in range(4):
+        turns[1, side] = turn_matrix(side, seam[1, side, me], seam[2, side, me], True)
     rims = strips_in(turns.at[1], rows, d_recv, tile_sems.at[3])
     grad[8:16, 8:56, :] += rims[0].reshape(8, 48, 64)
     grad[48:56, 8:56, :] += rims[1].reshape(8, 48, 64)
@@ -358,15 +393,15 @@
         return carry
 
     lax.fori_loop(0, 6, shallow_step, 0)
-    blank = jnp.zeros((64, 122), F32)
+    blank = jnp.zeros((122, 64), F32)
     inner = [
-        jnp.concatenate([in_w[3 * a + b].astype(F32) for b in range(3)] + [blank], axis=1).astype(BF16)
+        jnp.concatenate([in_w[3 * a + b].astype(F32) for b in range(3)] + [blank], axis=0).astype(BF16)
         for a in range(3)
     ]
     for c in range(7):
         total = jnp.zeros((384, 128), F32)
         for a in range(3):
-            total += dot(shallow[8 * c + 8 - 4 * a : 8 * c + 16 - 4 * a].reshape(384, 64), inner[a])
+            total += dot(shallow[8 * c + 8 - 4 * a : 8 * c + 16 - 4 * a].reshape(384, 64), inner[a], NT)
         bands_t[:, 384 * c : 384 * c + 384] = total.T[0:8]
     taps = bands_t[...]
     centre, left, right = taps[2:4], taps[0:2], taps[4:6]
@@ -414,8 +449,8 @@
     own = jnp.zeros((16, 64), jnp.int32) - 1
     for member in range(4):
         for side in range(4):
-            peer = seam[4 * depth + member, side, 0]
-            held = jnp.where(lax.rem(peer, 4) == quarter, (peer // 4) * 4 + seam[4 * depth + member, side, 1], -1)
+            peer = seam[0, side, 4 * depth + member]
+            held = jnp.where(lax.rem(peer, 4) == quarter, (peer // 4) * 4 + seam[1, side, 4 * depth + member], -1)
             own = jnp.where(row_of == 4 * member + side, held, own)
     chosen = jnp.where(own == iota((16, 64), 1), 1.0, 0.0).astype(BF16)
     active = jnp.where(panel[me] < 6, 1.0, 0.0)
@@ -469,18 +504,20 @@
 ):
     vmem = pl.BlockSpec(memory_space=pltpu.VMEM)
     smem = pl.BlockSpec(memory_space=pltpu.SMEM)
+    hbm = pl.BlockSpec(memory_space=pl.ANY)
+    seam_t = jnp.transpose(seam_list, (2, 1, 0))
     pieces = pltpu.VMEM((3, TILES, 4, 128), BF16)
     return pl.pallas_call(
         kernel,
         out_shape=jax.ShapeDtypeStruct((1, 1, 2, 2304), F32),
-        in_specs=[vmem, vmem, vmem, vmem, vmem, smem, vmem, vmem, smem, vmem, smem],
+        in_specs=[hbm, vmem, vmem, hbm, vmem, smem, vmem, vmem, smem, vmem, smem],
         out_specs=vmem,
         scratch_shapes=[
             pltpu.VMEM((48, 48, 64), F32),
             pltpu.VMEM((64, 64, 64), F32),
             pltpu.VMEM((64, 48, 192), BF16),
             pltpu.VMEM((6, 384, 64), BF16),
-            pltpu.VMEM((6, 384, 64), F32),
+            pltpu.VMEM((48, 48, 64), F32),
             pltpu.VMEM((6, 384, 64), F32),
             pltpu.VMEM((80, 64, 192), BF16),
             pltpu.VMEM((64, 64, 64), F32),
@@ -489,7 +526,7 @@
             pltpu.VMEM((2, 4, 384, 384), BF16),
             pltpu.VMEM((768, 2304), BF16),
             pltpu.VMEM((3, 256, 128), F32),
-            pltpu.VMEM((256, 3), jnp.int32),
+            pltpu.VMEM((256, 128), jnp.int32),
             pltpu.VMEM((256, 256), BF16),
         ]
         + [pieces] * 8
@@ -504,14 +541,17 @@
             pltpu.SemaphoreType.DMA((6, 2)),
             pltpu.SemaphoreType.DMA((6, 2)),
             pltpu.SemaphoreType.DMA((2, 2)),
+            pltpu.VMEM((1, 1, 64, 2304), BF16),
+            pltpu.VMEM((9, 64, 64), BF16),
+            pltpu.SemaphoreType.DMA((2,)),
         ],
         compiler_params=pltpu.CompilerParams(
-            collective_id=0, has_side_effects=True, vmem_limit_bytes=48 * 2**20
+            collective_id=0, has_side_effects=True, vmem_limit_bytes=62 * 2**20
         ),
         name="adjoint",
     )(
-        pre_act, cotangent.reshape(6, 1, 384), input_weight, conv_weight, down_weight, level_mix, up_weight,
-        head_weight.reshape(1, 64), seam_list, seam_list, tile_panel,
+        pre_act, cotangent.reshape(6, 1, 384), jnp.transpose(input_weight, (0, 2, 1)), conv_weight, down_weight,
+        level_mix, up_weight.T, head_weight.reshape(1, 64), seam_t, seam_t, tile_panel,
     )
 
 

time: 102 us -> 94.9 us (0.930)
  Pallas kernels: 97.6 us -> 93.4 us
  local copies, waits for them, and re-layouts: 4.06 us -> 1.33 us
    pallas_call x1, Pallas kernels: 97.6 us -> 93.4 us  [shards(): pl.pallas_call(kernel, out_shape=jax.ShapeDtypeStruct((1, 1, 2, 2304), F3...]
    unnamed x18 -> x1, local copies, waits for them, and re-layouts: 4.06 us -> 1.33 us
where the time goes in v3:
time: 94.9 us; the launch traced here: 94.7 us
  Pallas kernels  93.4 us (98%)
  local copies, waits for them, and re-layouts  1.33 us (1%)
    pallas_call x1, Pallas kernels, shards(): pl.pallas_call(kernel, out_shape=jax.ShapeDtypeStruct((1, 1, 2, 2304), F3...  93.4 us

profile of v3, /device:TPU:1, one launch (start us, length us, event | category | flops | bytes accessed | tf_op | source)
XLA Modules:
  0.0 94.7 jit_solution(2828954264664039772)
XLA Ops:
  0.0 93.4 %adjoint.1 = f32[1,1,2,2304]{3,2,1,0:T(2,128)} custom-call(bf16[1,1,64,2304]{3,2,1,0:T(8,128)(2,1)} %pre_hbm.1, bf16[6,1,384]{2,1,0:T(2,128)(2,1)} %bitcast.7, bf16[9,2,64]{2,1,0:T(2,128)(2,1)} %bitcast.8, bf16[9,64,64]{2,1,0:T(8,128)(2,1)} %conv_hbm.1, bf16[8,64]{1,0:T(8,128)(2,1)} %down_ref.1, f32[8,8]{1,0:T(8,128)} %mix_ref.1, bf16[8,64]{1,0:T(8,128)(2,1)} %bitcast.9, ...), custom_call_target="tpu_custom_call" | custom-call | tf_op jit(solution)/shard_map/adjoint/pallas_call | solution.py:510
  93.4 1.3 %copy.12 = f32[1,1,2,2304]{3,2,1,0:T(2,128)} copy(f32[1,1,2,2304]{3,2,1,0:T(2,128)} %adjoint.1) | data formatting | bytes 36864

commit v4 on v3

--- a/solution.py
+++ b/solution.py
@@ -114,12 +114,50 @@
     return [dot(turns[side], slab_from_rows(rows, side).astype(BF16)) for side in range(4)]
 
 
-def level_start(buf, c, sems, level):
+def level_start(buf, sems, level):
     for i in (4, 3, 5, 2, 6, 1, 7):
         pltpu.make_async_remote_copy(
-            buf.at[c, level], buf.at[c, level], sems.at[c, 0], sems.at[c, 1],
+            buf.at[level], buf.at[level], sems.at[0], sems.at[1],
             device_id={"lev": jnp.bitwise_and(level + i, LEVS - 1)}, device_id_type=MESH,
         ).start()
+
+
+CELLS = (384, 384, 512, 512, 512)
+
+
+def load_group(ref, k, first=0):
+    if k < 2:
+        return ref[first + 40 * k : first + 40 * k + 8].reshape(384, 64)
+    if k == 2:
+        middle = slice(first + 8, first + 40)
+        return jnp.concatenate(
+            [ref[middle, 0:8, :].reshape(256, 64), ref[middle, 40:48, :].reshape(256, 64)], axis=0
+        )
+    row = first + 8 + 16 * (k - 3)
+    return ref[row : row + 16, 8:40, :].reshape(512, 64)
+
+
+def store_group(ref, k, value, first=0):
+    if k < 2:
+        ref[first + 40 * k : first + 40 * k + 8] = value.reshape(8, 48, 64)
+    elif k == 2:
+        ref[first + 8 : first + 40, 0:8, :] = value[0:256].reshape(32, 8, 64)
+        ref[first + 8 : first + 40, 40:48, :] = value[256:512].reshape(32, 8, 64)
+    else:
+        row = first + 8 + 16 * (k - 3)
+        ref[row : row + 16, 8:40, :] = value.reshape(16, 32, 64)
+
+
+def columns_joined(d):
+    edge = jnp.zeros((8, 8, 64), F32)
+    return jnp.concatenate(
+        [
+            jnp.concatenate([d[:, 8:48], edge], axis=1),
+            d,
+            jnp.concatenate([edge, d[:, 0:40]], axis=1),
+        ],
+        axis=2,
+    ).astype(BF16)
 
 
 def turn_matrix(side, edge, flip, of_bands):
@@ -144,8 +182,8 @@
 
 def kernel(
     pre_hbm, cot_ref, in_w, conv_hbm, down_ref, mix_ref, up_ref, head_ref, seam, seam_v, panel, out_ref,
-    pre_t, padded, wide, act, second, top, deep_wide, grad, shallow, bands_t, turns, place, rows, wanted,
-    choice, a_send, a_recv, b_send, b_recv, c_send, c_recv, d_send, d_recv, e_send, e_recv, f_send, f_recv, lat, glat,
+    pre_t, padded, wide, act, second, top, gain, deep, deep_wide, grad, bands, shallow, bands_t, turns, place, rows, wanted,
+    choice, a_send, a_recv, b_send, b_recv, c_send, c_recv, d_send, d_recv, e_send, e_recv, f_send, f_recv, lat_a, lat_b, glat_a, glat_b,
     tile_sems, lat_sems, glat_sems, last_sems, pre_ref, conv_w, load_sems,
 ):
     me = lax.axis_index("tile")
@@ -163,6 +201,42 @@
     lax.fori_loop(1, TILES, greet, 0)
     for i in range(1, LEVS):
         pl.semaphore_signal(barrier, inc=1, device_id={"lev": lax.rem(level + i, LEVS)}, device_id_type=MESH)
+
+    down = down_ref[...]
+    up_t = up_ref[...]
+
+    def squash(k):
+        total = load_group(second, k)
+        s = (total * jax.nn.sigmoid(total)).astype(BF16)
+        act[k, 0 : CELLS[k]] = s
+        buf = lat_a.at[k] if k < 2 else lat_b.at[k - 2]
+        buf[level] = dot(down, s, NT).astype(BF16)
+        level_start(buf, lat_sems.at[k], level)
+
+    def top_step(k):
+        buf = lat_a.at[k] if k < 2 else lat_b.at[k - 2]
+        arrived_all(buf, LEVS - 1, lat_sems.at[k, 1])
+        mixed = mix_ref[level, 0] * buf[0].astype(F32)
+        for other in range(1, LEVS):
+            mixed += mix_ref[level, other] * buf[other].astype(F32)
+        mixed = mixed.astype(BF16).astype(F32).T.astype(BF16)
+        third = act[k, 0 : CELLS[k]].astype(F32) + dot(mixed, up_t)
+        gradient = load_group(gain, k) * dsilu(third)
+        top[k, 0 : CELLS[k]] = gradient
+        out = glat_a.at[k] if k < 2 else glat_b.at[k - 2]
+        out[level] = dot(up_t, gradient.astype(BF16), NT).astype(BF16)
+        level_start(out, glat_sems.at[k], level)
+
+    def deep_step(k):
+        buf = glat_a.at[k] if k < 2 else glat_b.at[k - 2]
+        arrived_all(buf, LEVS - 1, glat_sems.at[k, 1])
+        mixed = mix_ref[0, level] * buf[0].astype(F32)
+        for other in range(1, LEVS):
+            mixed += mix_ref[other, level] * buf[other].astype(F32)
+        mixed = mixed.astype(BF16).astype(F32).T.astype(BF16)
+        gradient = top[k, 0 : CELLS[k]] + dot(mixed, down)
+        d = gradient * dsilu(load_group(second, k))
+        store_group(deep, k, d.astype(BF16).astype(F32), 8)
 
     load_pre.wait()
     pre_t[...] = pre_ref[0, 0].astype(F32).T.reshape(48, 48, 64)
@@ -214,8 +288,6 @@
         return carry
 
     lax.fori_loop(1, 7, widen, 0)
-    down = down_ref[...]
-    up_t = up_ref[...]
     forward = [
         jnp.concatenate([conv_w[3 * a + b] for b in range(3)], axis=1) for a in range(3)
     ]
@@ -229,11 +301,8 @@
 
     lax.fori_loop(0, 6, conv, 0)
 
-    strips_on(choice, rows, a_recv, tile_sems.at[0], b_send, b_recv, tile_sems.at[1], me)
-
-    for side in range(4):
-        turns[0, side] = turn_matrix(side, seam[1, side, me], seam[2, side, me], False)
-
+    squash(3)
+    squash(4)
     head = head_ref[...]
     high = head.astype(BF16)
     rest = head - high.astype(F32)
@@ -244,15 +313,27 @@
         [high.astype(F32), middle.astype(F32), low.astype(F32), zero_rows], axis=0
     ).astype(BF16)
 
-    def clear(c, carry):
-        deep_wide[pl.ds(8 * c, 8)] = jnp.zeros((8, 64, 192), BF16)
-        deep_wide[pl.ds(64 + 8 * c, 8)] = jnp.zeros((8, 64, 192), BF16)
-        return carry
-
-    lax.fori_loop(0, 2, clear, 0)
+    def scale(c, carry):
+        cot = jnp.broadcast_to(cot_ref[c].astype(F32), (8, 384)).T.astype(BF16)
+        gain[pl.ds(8 * c, 8)] = dot(cot, heads).reshape(8, 48, 64)
+        return carry
+
+    lax.fori_loop(0, 6, scale, 0)
+    strips_on(choice, rows, a_recv, tile_sems.at[0], b_send, b_recv, tile_sems.at[1], me)
+
+    for side in range(4):
+        turns[0, side] = turn_matrix(side, seam[1, side, me], seam[2, side, me], False)
+
+    top_step(3)
+    top_step(4)
+    deep[0:8] = jnp.zeros((8, 48, 64), F32)
+    deep[56:64] = jnp.zeros((8, 48, 64), F32)
+    deep_wide[0:8] = jnp.zeros((8, 48, 192), BF16)
+    deep_wide[56:64] = jnp.zeros((8, 48, 192), BF16)
     shallow[0:8] = jnp.zeros((8, 48, 64), BF16)
     shallow[56:64] = jnp.zeros((8, 48, 64), BF16)
-
+    deep_step(3)
+    deep_step(4)
     rims = strips_in(turns.at[0], rows, b_recv, tile_sems.at[1])
     edge = jnp.zeros((8, 8, 64), F32)
     for side, a in ((0, 0), (1, 2)):
@@ -274,77 +355,40 @@
             extra += dot(rim[8 * a : 8 * a + 48].reshape(384, 64).astype(BF16), conv_w[3 * a + b], NT)
         second[:, 20 * b : 20 * b + 8, :] += extra.reshape(48, 8, 64)
 
-    def squash(c, carry):
-        total = second[pl.ds(8 * c, 8)].reshape(384, 64)
-        s = (total * jax.nn.sigmoid(total)).astype(BF16)
-        act[c] = s
-        lat[c, level] = dot(down, s, NT).astype(BF16)
-        level_start(lat, c, lat_sems, level)
-        return carry
-
-    lax.fori_loop(0, 6, squash, 0)
-
-    def top_step(c, carry):
-        arrived_all(lat.at[c], LEVS - 1, lat_sems.at[c, 1])
-        mixed = mix_ref[level, 0] * lat[c, 0].astype(F32)
-        for other in range(1, LEVS):
-            mixed += mix_ref[level, other] * lat[c, other].astype(F32)
-        mixed = mixed.astype(BF16).astype(F32).T.astype(BF16)
-        third = act[c].astype(F32) + dot(mixed, up_t)
-        cot = jnp.broadcast_to(cot_ref[c].astype(F32), (8, 384)).T.astype(BF16)
-        gradient = dot(cot, heads) * dsilu(third)
-        top[c] = gradient
-        glat[c, level] = dot(up_t, gradient.astype(BF16), NT).astype(BF16)
-        level_start(glat, c, glat_sems, level)
-        return carry
-
-
-    lax.fori_loop(0, 6, top_step, 0)
-
-    def deep_step(c, carry):
-        arrived_all(glat.at[c], LEVS - 1, glat_sems.at[c, 1])
-        mixed = mix_ref[0, level] * glat[c, 0].astype(F32)
-        for other in range(1, LEVS):
-            mixed += mix_ref[other, level] * glat[c, other].astype(F32)
-        mixed = mixed.astype(BF16).astype(F32).T.astype(BF16)
-        gradient = top[c] + dot(mixed, down)
-        d = (gradient * dsilu(second[pl.ds(8 * c, 8)].reshape(384, 64))).reshape(8, 48, 64)
-        z8 = jnp.zeros((8, 8, 64), F32)
-        z16 = jnp.zeros((8, 16, 64), F32)
-        joined = jnp.concatenate(
-            [
-                jnp.concatenate([d, z16], axis=1),
-                jnp.concatenate([z8, d, z8], axis=1),
-                jnp.concatenate([z16, d], axis=1),
-            ],
-            axis=2,
-        )
-        deep_wide[pl.ds(8 * c + 16, 8)] = joined.astype(BF16)
-        return carry
-
-    lax.fori_loop(0, 6, deep_step, 0)
+    for k in range(3):
+        squash(k)
+    for k in range(3):
+        top_step(k)
+    for k in range(3):
+        deep_step(k)
     backward = [conv_w[3 * a : 3 * a + 3].reshape(192, 64) for a in range(3)]
-
-    grad[0:8] = dot(deep_wide[16:24].reshape(512, 192), backward[0]).reshape(8, 64, 64)
-    grad[56:64] = dot(deep_wide[56:64].reshape(512, 192), backward[2]).reshape(8, 64, 64)
-    for near, far, take in ((0, 0, 0), (48, 56, 8)):
-        total = jnp.zeros((768, 64), F32)
+    bands[0] = dot(columns_joined(deep[8:16]).reshape(384, 192), backward[0])
+    bands[1] = dot(columns_joined(deep[48:56]).reshape(384, 192), backward[2])
+    for side, b in ((2, 0), (3, 2)):
+        total = jnp.zeros((384, 64), F32)
         for a in range(3):
-            start = 8 * (3 - a)
-            total += dot(deep_wide[start : start + 48, near : near + 16, :].reshape(768, 192), backward[a])
-        grad[8:56, far : far + 8, :] = total.reshape(48, 16, 64)[:, take : take + 8]
+            here = deep[16 - 8 * a : 64 - 8 * a, 20 * b : 20 * b + 8, :].reshape(384, 64)
+            total += dot(here.astype(BF16), conv_w[3 * a + b])
+        bands[side] = total
     strips_out(
-        edges_of(grad, [(0, 8), (56, 8), (8, 0), (8, 56)]), rows, c_send, c_recv, tile_sems.at[2], me
+        [lambda j, side=side: bands[side, 128 * j : 128 * j + 128] for side in range(4)],
+        rows, c_send, c_recv, tile_sems.at[2], me,
     )
 
+    def spread(c, carry):
+        deep_wide[pl.ds(8 * c + 8, 8)] = columns_joined(deep[pl.ds(8 * c + 8, 8)])
+        return carry
+
+    lax.fori_loop(0, 6, spread, 0)
+
     def adjoint(c, carry):
-        total = jnp.zeros((512, 64), F32)
+        total = jnp.zeros((384, 64), F32)
         for a in range(3):
-            total += dot(deep_wide[pl.ds(8 * (c + 2 - a), 8)].reshape(512, 192), backward[a])
-        grad[pl.ds(8 * c, 8), 8:56, :] = total.reshape(8, 64, 64)[:, 8:56]
-        return carry
-
-    lax.fori_loop(1, 7, adjoint, 0)
+            total += dot(deep_wide[pl.ds(8 * (c + 2 - a), 8)].reshape(384, 192), backward[a])
+        grad[pl.ds(8 * c, 8)] = total.reshape(8, 48, 64)
+        return carry
+
+    lax.fori_loop(0, 6, adjoint, 0)
 
     def slope(c, carry):
         pre_t[pl.ds(8 * c, 8)] = dsilu(pre_t[pl.ds(8 * c, 8)])
@@ -381,14 +425,14 @@
     for side in range(4):
         turns[1, side] = turn_matrix(side, seam[1, side, me], seam[2, side, me], True)
     rims = strips_in(turns.at[1], rows, d_recv, tile_sems.at[3])
-    grad[8:16, 8:56, :] += rims[0].reshape(8, 48, 64)
-    grad[48:56, 8:56, :] += rims[1].reshape(8, 48, 64)
-    grad[8:56, 8:16, :] += rims[2].reshape(48, 8, 64)
-    grad[8:56, 48:56, :] += rims[3].reshape(48, 8, 64)
+    grad[0:8] += rims[0].reshape(8, 48, 64)
+    grad[40:48] += rims[1].reshape(8, 48, 64)
+    grad[:, 0:8, :] += rims[2].reshape(48, 8, 64)
+    grad[:, 40:48, :] += rims[3].reshape(48, 8, 64)
 
     def shallow_step(c, carry):
         shallow[pl.ds(8 * c + 8, 8)] = (
-            grad[pl.ds(8 * c + 8, 8), 8:56, :] * pre_t[pl.ds(8 * c, 8)]
+            grad[pl.ds(8 * c, 8)] * pre_t[pl.ds(8 * c, 8)]
         ).astype(BF16)
         return carry
 
@@ -491,9 +535,9 @@
     for phase, buf in enumerate((a_send, b_send, c_send, d_send)):
         for j in range(3):
             arrived_all(buf.at[j], TILES - 1, tile_sems.at[phase, j, 0])
-    for c in range(6):
-        arrived_all(lat.at[c], LEVS - 1, lat_sems.at[c, 0])
-        arrived_all(glat.at[c], LEVS - 1, glat_sems.at[c, 0])
+    for k in range(5):
+        arrived_all(lat_a.at[k] if k < 2 else lat_b.at[k - 2], LEVS - 1, lat_sems.at[k, 0])
+        arrived_all(glat_a.at[k] if k < 2 else glat_b.at[k - 2], LEVS - 1, glat_sems.at[k, 0])
     arrived_all(e_recv, 15, last_sems.at[0, 0])
     arrived_all(f_send, 3, last_sems.at[1, 0])
 
@@ -516,11 +560,14 @@
             pltpu.VMEM((48, 48, 64), F32),
             pltpu.VMEM((64, 64, 64), F32),
             pltpu.VMEM((64, 48, 192), BF16),
-            pltpu.VMEM((6, 384, 64), BF16),
+            pltpu.VMEM((5, 512, 64), BF16),
             pltpu.VMEM((48, 48, 64), F32),
-            pltpu.VMEM((6, 384, 64), F32),
-            pltpu.VMEM((80, 64, 192), BF16),
-            pltpu.VMEM((64, 64, 64), F32),
+            pltpu.VMEM((5, 512, 64), F32),
+            pltpu.VMEM((48, 48, 64), F32),
+            pltpu.VMEM((64, 48, 64), F32),
+            pltpu.VMEM((64, 48, 192), BF16),
+            pltpu.VMEM((48, 48, 64), F32),
+            pltpu.VMEM((4, 384, 64), F32),
             pltpu.VMEM((64, 48, 64), BF16),
             pltpu.VMEM((8, 2688), F32),
             pltpu.VMEM((2, 4, 384, 384), BF16),
@@ -535,11 +582,13 @@
             pltpu.VMEM((16, 3, 4, 128), BF16),
             pltpu.VMEM((4, 3, 4, 128), BF16),
             pltpu.VMEM((4, 3, 4, 128), BF16),
-            pltpu.VMEM((6, LEVS, 8, 384), BF16),
-            pltpu.VMEM((6, LEVS, 8, 384), BF16),
+            pltpu.VMEM((2, LEVS, 8, 384), BF16),
+            pltpu.VMEM((3, LEVS, 8, 512), BF16),
+            pltpu.VMEM((2, LEVS, 8, 384), BF16),
+            pltpu.VMEM((3, LEVS, 8, 512), BF16),
             pltpu.SemaphoreType.DMA((4, 3, 2)),
-            pltpu.SemaphoreType.DMA((6, 2)),
-            pltpu.SemaphoreType.DMA((6, 2)),
+            pltpu.SemaphoreType.DMA((5, 2)),
+            pltpu.SemaphoreType.DMA((5, 2)),
             pltpu.SemaphoreType.DMA((2, 2)),
             pltpu.VMEM((1, 1, 64, 2304), BF16),
             pltpu.VMEM((9, 64, 64), BF16),

time: 94.9 us -> 93.7 us (0.987)
  Pallas kernels: 93.4 us -> 92.2 us
    pallas_call x1, Pallas kernels: 93.4 us -> 92.2 us  [shards(): pl.pallas_call(kernel, out_shape=jax.ShapeDtypeStruct((1, 1, 2, 2304), F3...]
where the time goes in v4:
time: 93.7 us; the launch traced here: 93.5 us
  Pallas kernels  92.2 us (98%)
  local copies, waits for them, and re-layouts  1.33 us (1%)
    pallas_call x1, Pallas kernels, shards(): pl.pallas_call(kernel, out_shape=jax.ShapeDtypeStruct((1, 1, 2, 2304), F3...  92.2 us

profile of v4, /device:TPU:1, one launch (start us, length us, event | category | flops | bytes accessed | tf_op | source)
XLA Modules:
  0.0 93.5 jit_solution(13902868701319429033)
XLA Ops:
  0.0 92.2 %adjoint.1 = f32[1,1,2,2304]{3,2,1,0:T(2,128)} custom-call(bf16[1,1,64,2304]{3,2,1,0:T(8,128)(2,1)} %pre_hbm.1, bf16[6,1,384]{2,1,0:T(2,128)(2,1)} %bitcast.7, bf16[9,2,64]{2,1,0:T(2,128)(2,1)} %bitcast.8, bf16[9,64,64]{2,1,0:T(8,128)(2,1)} %conv_hbm.1, bf16[8,64]{1,0:T(8,128)(2,1)} %down_ref.1, f32[8,8]{1,0:T(8,128)} %mix_ref.1, bf16[8,64]{1,0:T(8,128)(2,1)} %bitcast.9, ...), custom_call_target="tpu_custom_call" | custom-call | tf_op jit(solution)/shard_map/adjoint/pallas_call | solution.py:554
  92.2 1.3 %copy.12 = f32[1,1,2,2304]{3,2,1,0:T(2,128)} copy(f32[1,1,2,2304]{3,2,1,0:T(2,128)} %adjoint.1) | data formatting | bytes 36864

commit v5 on v4

--- a/solution.py
+++ b/solution.py
@@ -63,26 +63,19 @@
     rows[j, pl.ds(member, 64, stride=4), :] = jnp.concatenate([slab[0:64], slab[64:128]], axis=1)
 
 
-def slab_from_rows(rows, member):
-    parts = []
-    for j in range(3):
-        block = rows[j, pl.ds(member, 64, stride=4), :]
-        parts += [block[:, :64], block[:, 64:]]
-    return jnp.concatenate(parts, axis=0)
-
-
 def spread_start(send, recv, sems, me):
     recv[me] = send[me]
 
     def step(i, carry):
-        target = peer_at(me, i)
-        pltpu.make_async_remote_copy(
-            send.at[target], recv.at[me], sems.at[0], sems.at[1],
-            device_id={"tile": target}, device_id_type=MESH,
-        ).start()
-        return carry
-
-    lax.fori_loop(1, TILES, step, 0)
+        for k in range(1, 4):
+            target = peer_at(me, 3 * i + k)
+            pltpu.make_async_remote_copy(
+                send.at[target], recv.at[me], sems.at[0], sems.at[1],
+                device_id={"tile": target}, device_id_type=MESH,
+            ).start()
+        return carry
+
+    lax.fori_loop(0, (TILES - 1) // 3, step, 0)
 
 
 def arrived_all(ref, count, sem):
@@ -90,12 +83,10 @@
     pltpu.make_async_copy(some, some, sem).wait()
 
 
-def strips_out(slabs, rows, send, recv, sems, me):
-    for j in range(3):
-        for member in range(4):
-            slab_to_rows(rows, j, member, slabs[member](j))
-        pieces_from_rows(send.at[j], rows, j)
-        spread_start(send.at[j], recv.at[j], sems.at[j], me)
+def strips_cut(slabs, rows, send, j):
+    for member in range(4):
+        slab_to_rows(rows, j, member, slabs[member](j))
+    pieces_from_rows(send.at[j], rows, j)
 
 
 def strips_on(choice, rows, first_recv, first_sems, send, recv, sems, me):
@@ -107,11 +98,15 @@
         spread_start(send.at[j], recv.at[j], sems.at[j], me)
 
 
-def strips_in(turns, rows, recv, sems):
+def strips_in(turns, rows, rims, recv, sems):
     for j in range(3):
         arrived_all(recv.at[j], TILES - 1, sems.at[j, 1])
         rows_from_pieces(rows, j, recv.at[j])
-    return [dot(turns[side], slab_from_rows(rows, side).astype(BF16)) for side in range(4)]
+        for side in range(4):
+            block = rows[j, pl.ds(side, 64, stride=4), :]
+            cells = jnp.concatenate([block[:, :64], block[:, 64:]], axis=0).astype(BF16)
+            part = dot(turns[side, :, 128 * j : 128 * j + 128], cells)
+            rims[side] = part if j == 0 else rims[side] + part
 
 
 def level_start(buf, sems, level):
@@ -182,7 +177,7 @@
 
 def kernel(
     pre_hbm, cot_ref, in_w, conv_hbm, down_ref, mix_ref, up_ref, head_ref, seam, seam_v, panel, out_ref,
-    pre_t, padded, wide, act, second, top, gain, deep, deep_wide, grad, bands, shallow, bands_t, turns, place, rows, wanted,
+    pre_t, padded, wide, act, second, top, gain, deep, deep_wide, grad, bands, rims, shallow, bands_t, turns, place, rows, wanted,
     choice, a_send, a_recv, b_send, b_recv, c_send, c_recv, d_send, d_recv, e_send, e_recv, f_send, f_recv, lat_a, lat_b, glat_a, glat_b,
     tile_sems, lat_sems, glat_sems, last_sems, pre_ref, conv_w, load_sems,
 ):
@@ -250,8 +245,6 @@
         return carry
 
     lax.fori_loop(0, 6, first, 0)
-    pl.semaphore_wait(barrier, TILES - 1 + LEVS - 1)
-
     def edges_of(ref, places):
         def rows_at(r, c0):
             return lambda j: ref[r : r + 8, c0 : c0 + 48, :].reshape(384, 64)[128 * j : 128 * j + 128]
@@ -261,9 +254,12 @@
 
         return [rows_at(*places[0]), rows_at(*places[1]), columns_at(*places[2]), columns_at(*places[3])]
 
-    strips_out(
-        edges_of(padded, [(8, 8), (48, 8), (8, 8), (8, 48)]), rows, a_send, a_recv, tile_sems.at[0], me
-    )
+    sides = edges_of(padded, [(8, 8), (48, 8), (8, 8), (8, 48)])
+    for j in range(3):
+        strips_cut(sides, rows, a_send, j)
+    pl.semaphore_wait(barrier, TILES - 1 + LEVS - 1)
+    for j in range(3):
+        spread_start(a_send.at[j], a_recv.at[j], tile_sems.at[0, j], me)
 
     wished = (seam_v[0] * 4 + seam_v[1]).astype(F32)
     wished = jnp.concatenate([wished, jnp.zeros((4, 64), F32)], axis=0)
@@ -334,7 +330,7 @@
     shallow[56:64] = jnp.zeros((8, 48, 64), BF16)
     deep_step(3)
     deep_step(4)
-    rims = strips_in(turns.at[0], rows, b_recv, tile_sems.at[1])
+    strips_in(turns.at[0], rows, rims, b_recv, tile_sems.at[1])
     edge = jnp.zeros((8, 8, 64), F32)
     for side, a in ((0, 0), (1, 2)):
         rim = rims[side].reshape(8, 48, 64)
@@ -370,10 +366,10 @@
             here = deep[16 - 8 * a : 64 - 8 * a, 20 * b : 20 * b + 8, :].reshape(384, 64)
             total += dot(here.astype(BF16), conv_w[3 * a + b])
         bands[side] = total
-    strips_out(
-        [lambda j, side=side: bands[side, 128 * j : 128 * j + 128] for side in range(4)],
-        rows, c_send, c_recv, tile_sems.at[2], me,
-    )
+    sides = [lambda j, side=side: bands[side, 128 * j : 128 * j + 128] for side in range(4)]
+    for j in range(3):
+        strips_cut(sides, rows, c_send, j)
+        spread_start(c_send.at[j], c_recv.at[j], tile_sems.at[2, j], me)
 
     def spread(c, carry):
         deep_wide[pl.ds(8 * c + 8, 8)] = columns_joined(deep[pl.ds(8 * c + 8, 8)])
@@ -424,7 +420,7 @@
     strips_on(choice, rows, c_recv, tile_sems.at[2], d_send, d_recv, tile_sems.at[3], me)
     for side in range(4):
         turns[1, side] = turn_matrix(side, seam[1, side, me], seam[2, side, me], True)
-    rims = strips_in(turns.at[1], rows, d_recv, tile_sems.at[3])
+    strips_in(turns.at[1], rows, rims, d_recv, tile_sems.at[3])
     grad[0:8] += rims[0].reshape(8, 48, 64)
     grad[40:48] += rims[1].reshape(8, 48, 64)
     grad[:, 0:8, :] += rims[2].reshape(48, 8, 64)
@@ -568,6 +564,7 @@
             pltpu.VMEM((64, 48, 192), BF16),
             pltpu.VMEM((48, 48, 64), F32),
             pltpu.VMEM((4, 384, 64), F32),
+            pltpu.VMEM((4, 384, 64), F32),
             pltpu.VMEM((64, 48, 64), BF16),
             pltpu.VMEM((8, 2688), F32),
             pltpu.VMEM((2, 4, 384, 384), BF16),

time: 93.7 us -> 92.9 us (level)
  no operation moved by 1% of the time
where the time goes in v5:
time: 92.9 us; the launch traced here: 92.7 us
  Pallas kernels  91.3 us (98%)
  local copies, waits for them, and re-layouts  1.33 us (1%)
    pallas_call x1, Pallas kernels, shards(): pl.pallas_call(kernel, out_shape=jax.ShapeDtypeStruct((1, 1, 2, 2304), F3...  91.3 us

profile of v5, /device:TPU:1, one launch (start us, length us, event | category | flops | bytes accessed | tf_op | source)
XLA Modules:
  0.0 92.7 jit_solution(12562398888959489191)
XLA Ops:
  0.0 91.3 %adjoint.1 = f32[1,1,2,2304]{3,2,1,0:T(2,128)} custom-call(bf16[1,1,64,2304]{3,2,1,0:T(8,128)(2,1)} %pre_hbm.1, bf16[6,1,384]{2,1,0:T(2,128)(2,1)} %bitcast.7, bf16[9,2,64]{2,1,0:T(2,128)(2,1)} %bitcast.8, bf16[9,64,64]{2,1,0:T(8,128)(2,1)} %conv_hbm.1, bf16[8,64]{1,0:T(8,128)(2,1)} %down_ref.1, f32[8,8]{1,0:T(8,128)} %mix_ref.1, bf16[8,64]{1,0:T(8,128)(2,1)} %bitcast.9, ...), custom_call_target="tpu_custom_call" | custom-call | tf_op jit(solution)/shard_map/adjoint/pallas_call | solution.py:550
  91.3 1.3 %copy.12 = f32[1,1,2,2304]{3,2,1,0:T(2,128)} copy(f32[1,1,2,2304]{3,2,1,0:T(2,128)} %adjoint.1) | data formatting | bytes 36864
